TPU v7x, 32 devices: a whole 2x2x4 slice. The times are simulated.
32 devices in a mesh: batch: 2 (over x), ctx: 4 (over z), tp: 4 (over y, core).
Axes of the slice: x: 2, y: 2, z: 4, core: 2. Of those that a mesh axis runs over, the one named last changes fastest.
Arguments:
- frames: bfloat16 [1536, 1536], P(('batch', 'ctx'), 'tp'), parts along dimension 0, may hold values from -6 to 6
- attn_gain: float32 [1536], replicated, may hold values from 0.5 to 1.5
- query_key_value: bfloat16 [3, 1536, 1536], P(None, None, 'tp'), may hold values from -1 to 1
- out_weight: bfloat16 [1536, 1536], P('tp'), may hold values from -6 to 6
- conv_gain: float32 [1536], replicated, may hold values from 0.5 to 1.5
- glu_weight: bfloat16 [2, 1536, 1536], P(None, None, 'tp'), may hold values from -0.15625 to 0.15625
- depth_kernel: bfloat16 [31, 1536], P(None, 'tp'), may hold values from -1 to 1
- depth_bias: float32 [1536], P('tp'), may hold values from -4 to 4
- proj_weight: bfloat16 [1536, 1536], P('tp'), may hold values from -0.15625 to 0.15625
Outputs:
- layer_out: bfloat16 [1536, 1536], P(('batch', 'ctx'), 'tp'), parts along dimension 0
There are 2 independent parts, one for each index of `batch`. A program takes and returns all parts, laid end to end along the dimension named above; an argument that names none is the same for every part. Nothing has to cross between parts.
All inputs are finite; a program needn't handle non-finite values.
Results may differ from a plain program's by a relative error of at most 0.019.
Values may be sent and summed in bfloat16 or wider, within the bound.
A program may use at most 128 MiB of HBM per device.

v0:
```python
import math

import jax
import jax.numpy as jnp
from jax import lax
from jax.sharding import PartitionSpec as P

HEAD = 96


def layer_norm(inputs, gain):
    inputs = inputs.astype(jnp.float32)
    average = jnp.mean(inputs, axis=-1, keepdims=True)
    centered = inputs - average
    variance = jnp.mean(centered * centered, axis=-1, keepdims=True)
    return (centered * lax.rsqrt(variance + 1e-05) * gain).astype(jnp.bfloat16)


def depthwise(padded, kernel, bias, count):
    convolved = jnp.zeros((count, padded.shape[1]), jnp.float32)
    for kernel_tap in range(kernel.shape[0]):
        convolved = convolved + padded[kernel_tap : kernel_tap + count].astype(
            jnp.float32
        ) * kernel[kernel_tap].astype(jnp.float32)
    return jax.nn.silu(convolved + bias).astype(jnp.bfloat16)


def per_device(
    frames,
    attn_gain,
    query_key_value,
    out_weight,
    conv_gain,
    glu_weight,
    depth_kernel,
    depth_bias,
    proj_weight,
):
    frame_rows = frames.shape[0]
    local_cols = frames.shape[1]
    heads_here = query_key_value.shape[2] // HEAD
    whole_rows = lax.all_gather(frames, "tp", axis=1, tiled=True)
    normed = layer_norm(whole_rows, attn_gain)
    projected = jnp.einsum(
        "td,gdc->gtc", normed, query_key_value, preferred_element_type=jnp.float32
    ).astype(jnp.bfloat16)
    score_scale = 1.0 / math.sqrt(HEAD)
    query_heads = projected[0].reshape(frame_rows, heads_here, HEAD)
    initial = (
        jnp.full((heads_here, frame_rows), -1e30, jnp.float32),
        jnp.zeros((heads_here, frame_rows), jnp.float32),
        jnp.zeros((frame_rows, heads_here, HEAD), jnp.float32),
    )
    pieces = (
        lax.all_gather(projected[1], "ctx", axis=0, tiled=True),
        lax.all_gather(projected[2], "ctx", axis=0, tiled=True),
    )
    key_count = pieces[0].shape[0]
    block_len = 1024 if key_count > 1024 and key_count % 1024 == 0 else key_count
    key_blocks = pieces[0].reshape(key_count // block_len, block_len, heads_here, HEAD)
    value_blocks = pieces[1].reshape(key_count // block_len, block_len, heads_here, HEAD)

    def one_block(running, pieces_now):
        running_max, denominator, weighted = running
        key_block, value_block = pieces_now
        scores = (
            jnp.einsum("qhd,khd->hqk", query_heads, key_block, preferred_element_type=jnp.float32)
            * score_scale
        )
        new_max = jnp.maximum(running_max, jnp.max(scores, axis=-1))
        weights = jnp.exp(scores - new_max[:, :, None])
        rescale = jnp.exp(running_max - new_max)
        denominator = denominator * rescale + jnp.sum(weights, axis=-1)
        added = jnp.einsum(
            "hqk,khd->qhd",
            weights.astype(jnp.bfloat16),
            value_block,
            preferred_element_type=jnp.float32,
        )
        weighted = weighted * jnp.transpose(rescale)[:, :, None] + added
        return ((new_max, denominator, weighted), None)

    result, _ = lax.scan(one_block, initial, (key_blocks, value_blocks))
    running_max, denominator, weighted = result
    context = (
        (weighted / jnp.transpose(denominator)[:, :, None])
        .reshape(frame_rows, local_cols)
        .astype(jnp.bfloat16)
    )
    attn_terms = jnp.dot(context, out_weight, preferred_element_type=jnp.float32)
    summed = lax.psum(attn_terms.astype(jnp.bfloat16), "tp").astype(jnp.float32)
    middle_whole = (whole_rows.astype(jnp.float32) + summed).astype(jnp.bfloat16)
    middle = lax.dynamic_slice_in_dim(
        middle_whole, lax.axis_index("tp") * local_cols, local_cols, 1
    )
    normed_conv = layer_norm(middle_whole, conv_gain)
    halves = jnp.einsum("td,gdc->gtc", normed_conv, glu_weight, preferred_element_type=jnp.float32)
    glu = (halves[0] * jax.nn.sigmoid(halves[1])).astype(jnp.bfloat16)
    reach = depth_kernel.shape[0] // 2
    regrouped = lax.all_to_all(glu, "ctx", split_axis=1, concat_axis=0, tiled=True)
    group_cols = regrouped.shape[1]
    offset_cols = lax.axis_index("ctx") * group_cols
    kernel_part = lax.dynamic_slice_in_dim(depth_kernel, offset_cols, group_cols, 1)
    bias_part = lax.dynamic_slice_in_dim(depth_bias, offset_cols, group_cols, 0)
    padded = jnp.pad(regrouped, ((reach, reach), (0, 0)))
    activated_part = depthwise(padded, kernel_part, bias_part, regrouped.shape[0])
    activated = lax.all_to_all(activated_part, "ctx", split_axis=0, concat_axis=1, tiled=True)
    conv_terms = jnp.dot(activated, proj_weight, preferred_element_type=jnp.float32)
    conv_sum = lax.psum_scatter(
        conv_terms.astype(jnp.bfloat16), "tp", scatter_dimension=1, tiled=True
    ).astype(jnp.float32)
    return (middle.astype(jnp.float32) + conv_sum).astype(jnp.bfloat16)


def solution(mesh):
    in_specs = (
        P(("batch", "ctx"), "tp"),
        P(),
        P(None, None, "tp"),
        P("tp", None),
        P(),
        P(None, None, "tp"),
        P(None, "tp"),
        P("tp"),
        P("tp", None),
    )
    out_specs = P(("batch", "ctx"), "tp")
    return jax.shard_map(
        per_device, mesh=mesh, in_specs=in_specs, out_specs=out_specs, check_vma=False
    )
```

profile of v0, /device:TPU:0, one launch (start us, length us, event | category | flops | bytes accessed | tf_op | source)
XLA Modules:
  0.0 179.0 jit_solution(11583778688881468693)
XLA Ops:
  6.5 9.3 %all_gather.9 = bf16[192,1536]{1,0:T(8,128)(2,1)S(1)} all-gather(bf16[192,384]{1,0:T(8,128)(2,1)} %param.9), channel_id=1, replica_groups=mesh['batch'=2,'ctx'=4,'tp'=4] {'tp'}, dimensions={1}, use_global_device_ids=true | all-gather | bytes 737280 | tf_op jit(solution)/shard_map/all_gather | solution.py:42
  18.1 17.5 %all-gather = bf16[1,768,384]{2,1,0:T(8,128)(2,1)} all-gather(bf16[1,192,384]{2,1,0:T(8,128)(2,1)S(1)} %get-tuple-element.28), channel_id=2, replica_groups=mesh['batch'=2,'ctx'=4,'tp'=4] {'ctx'}, dimensions={1}, use_global_device_ids=true | all-gather | bytes 737280 | tf_op jit(solution)/shard_map/all_gather | solution.py:55
  35.6 2.1 %copy.18 = bf16[1,768,384]{1,2,0:T(8,128)(2,1)} copy(bf16[1,768,384]{2,1,0:T(8,128)(2,1)} %all-gather) | data formatting | bytes 1179648 | tf_op jit(solution)/shard_map/all_gather | solution.py:55
  37.7 1.7 reshape_squeeze.3
  39.5 1.7 multiply_reduce_fusion
  42.6 16.6 %all-gather.1 = bf16[1,768,384]{2,1,0:T(8,128)(2,1)} all-gather(bf16[1,192,384]{2,1,0:T(8,128)(2,1)S(1)} %copy-done.5), channel_id=3, replica_groups=mesh['batch'=2,'ctx'=4,'tp'=4] {'ctx'}, dimensions={1}, use_global_device_ids=true | all-gather | bytes 737280 | tf_op jit(solution)/shard_map/all_gather | solution.py:56
  59.2 2.1 %copy.20 = bf16[1,768,384]{1,2,0:T(8,128)(2,1)} copy(bf16[1,768,384]{2,1,0:T(8,128)(2,1)} %all-gather.1) | data formatting | bytes 1179648 | tf_op jit(solution)/shard_map/all_gather | solution.py:56
  61.3 2.7 %fusion.19 = bf16[192,4,96]{0,2,1:T(8,128)(2,1)S(1)} fusion(bf16[768,4,96]{0,2,1:T(8,128)(2,1)} %bitcast.203, f32[4,192,768]{2,1,0:T(8,128)} %copy-done.2, f32[4,192]{1,0:T(4,128)S(1)} %get-tuple-element.63, f32[192,4]{0,1:T(4,128)S(1)} %bitcast_add_fusion, f32[192,4]{0,1:T(4,128)S(1)} %get-tuple-element.62), kind=kOutput, calls=%fused_computation.30 | convolution fusion | flops 115236864 | bytes 3105792 | tf_op jit(solution)/shard_map/while/body/eval_jaxpr/hqk,khd->qhd/dot_general | solution.py:74
  66.6 33.6 %all-reduce.3.cloned.1.call-done = bf16[192,1536]{1,0:T(8,128)(2,1)} async-done(((bf16[192,1536]{1,0:T(8,128)(2,1)}), bf16[192,1536]{1,0:T(8,128)(2,1)}) %all-reduce.3.cloned.1.call-update) | async-done | bytes 589840 | tf_op jit(solution)/shard_map/psum | solution.py:91
  103.7 1.7 copy.25
  105.4 4.6 %all-to-all-start = ((bf16[192,4,96]{0,2,1:T(8,128)(2,1)}), bf16[192,4,96]{0,2,1:T(8,128)(2,1)}, u32[]{:S(2)}, u32[]{:S(2)}) async-start(bf16[192,4,96]{0,2,1:T(8,128)(2,1)} %bitcast.201), calls=%async_computation | async-start | bytes 393216 | tf_op jit(solution)/shard_map/all_to_all | solution.py:100
  110.0 1.7 fusion.68
  111.7 1.8 fusion.69
  113.5 3.0 %all-to-all-done = bf16[192,4,96]{0,2,1:T(8,128)(2,1)} async-done(((bf16[192,4,96]{0,2,1:T(8,128)(2,1)}), bf16[192,4,96]{0,2,1:T(8,128)(2,1)}, u32[]{:S(2)}, u32[]{:S(2)}) %all-to-all-start) | async-done | bytes 147488 | tf_op jit(solution)/shard_map/all_to_all | solution.py:100
  116.5 1.8 copy.22
  118.3 1.8 all_to_all.28
  120.0 8.0 %multiply_convert_fusion = bf16[768,96]{0,1:T(8,128)(2,1)} fusion(bf16[768,96]{0,1:T(8,128)(2,1)} %all_to_all.28, f32[96]{0:T(128)} %dynamic_slice.16, f32[96]{0:T(128)} %get-tuple-element.61, f32[96]{0:T(128)S(1)} %get-tuple-element.32, f32[96]{0:T(128)S(1)} %get-tuple-element.33, f32[96]{0:T(128)S(1)} %get-tuple-element.34, f32[96]{0:T(128)} %get-tuple-element.35, ...), kind=kLoop, calls=%fused_computation.45 | loop fusion | flops 7225344 | bytes 307200 | tf_op jit(solution)/shard_map/convert_element_type | solution.py:25
  128.1 1.7 copy.26
  129.8 10.1 %all_to_all.35 = bf16[4,192,96]{2,1,0:T(8,128)(2,1)S(1)} all-to-all(bf16[4,192,96]{2,1,0:T(8,128)(2,1)} %bitcast.202), channel_id=1, replica_groups=mesh['batch'=2,'ctx'=4,'tp'=4] {'ctx'}, dimensions={0} | all-to-all | bytes 294912 | tf_op jit(solution)/shard_map/all_to_all | solution.py:107
  140.8 1.8 all_to_all.32
  142.5 2.7 %convolution_convert_fusion = bf16[192,1536]{1,0:T(8,128)(2,1)} fusion(bf16[192,384]{1,0:T(8,128)(2,1)} %all_to_all.32, bf16[384,1536]{1,0:T(8,128)(2,1)} %param.17), kind=kOutput, calls=%fused_computation | convolution fusion | flops 226787328 | bytes 1916928 | tf_op jit(solution)/shard_map/dot_general | solution.py:108
  145.2 2.2 %copy.27 = bf16[192,1536]{0,1:T(8,128)(2,1)} copy(bf16[192,1536]{1,0:T(8,128)(2,1)} %convolution_convert_fusion) | data formatting | bytes 1179648
  147.4 21.3 %reduce-scatter.4.cloned.1.call-done = bf16[384,192]{1,0:T(8,128)(2,1)} async-done(((bf16[1536,192]{1,0:T(8,128)(2,1)}), bf16[384,192]{1,0:T(8,128)(2,1)}) %reduce-scatter.4.cloned.1.call-update) | async-done | bytes 147472
  168.8 1.7 copy.28
  (41 shorter events, 12.2 us)
Async XLA Ops:
  6.5 9.8 %copy-start = (bf16[3,1536,384]{2,1,0:T(8,128)(2,1)S(1)}, bf16[3,1536,384]{2,1,0:T(8,128)(2,1)}, u32[]{:S(2)}) copy-start(bf16[3,1536,384]{2,1,0:T(8,128)(2,1)} %param.11) | copy-start | bytes 10616836
  6.5 9.8 %copy-start.7 = (f32[1536]{0:T(1024)S(1)}, f32[1536]{0:T(1024)}, u32[]{:S(2)}) copy-start(f32[1536]{0:T(1024)} %param.10) | copy-start | bytes 18436
  6.5 93.7 %all-reduce.3.cloned.1.call-start = ((), (), s32[]{:S(2)}) async-start(), calls=%async_computation.3 | async-start | bytes 1179648 | tf_op jit(solution)/shard_map/psum | solution.py:91
  15.9 1.5 copy-start.1
  41.2 1.4 copy-start.2
  41.2 1.4 copy-start.5
  61.3 2.7 %copy-start.4 = (bf16[384,1536]{1,0:T(8,128)(2,1)S(1)}, bf16[384,1536]{1,0:T(8,128)(2,1)}, u32[]{:S(2)}) copy-start(bf16[384,1536]{1,0:T(8,128)(2,1)} %param.12) | copy-start | bytes 3538948
  66.6 35.6 %copy-start.8 = (f32[1536]{0:T(1024)S(1)}, f32[1536]{0:T(1024)}, u32[]{:S(2)}) copy-start(f32[1536]{0:T(1024)} %param.13) | copy-start | bytes 18436
  100.2 2.0 %copy-start.6 = (bf16[2,1536,384]{2,1,0:T(8,128)(2,1)S(1)}, bf16[2,1536,384]{2,1,0:T(8,128)(2,1)}, u32[]{:S(2)}) copy-start(bf16[2,1536,384]{2,1,0:T(8,128)(2,1)} %param.14) | copy-start | bytes 7077892
  101.9 1.1 copy-start.3
  105.4 11.1 %all-to-all-start = ((bf16[192,4,96]{0,2,1:T(8,128)(2,1)}), bf16[192,4,96]{0,2,1:T(8,128)(2,1)}, u32[]{:S(2)}, u32[]{:S(2)}) async-start(bf16[192,4,96]{0,2,1:T(8,128)(2,1)} %bitcast.201), calls=%async_computation | async-start | bytes 393216 | tf_op jit(solution)/shard_map/all_to_all | solution.py:100
  110.0 58.7 %reduce-scatter.4.cloned.1.call-start = ((), (), s32[]{:S(2)}) async-start(), calls=%async_computation.4 | async-start | bytes 983040
Sparse Core Ops, SparseCore 0:
  65.5 34.7 all-reduce.2
  147.6 21.1 reduce-scatter.3
where the time goes:
time: 180 us; the launch traced here: 179 us
  waiting for transfers between devices  57.9 us (32%)
  blocking collectives  53.5 us (30%)
  local copies, waits for them, and re-layouts  22.3 us (12%)
  other arithmetic  17 us (9%)
  between operations  13.5 us (8%)
  matrix products  10 us (6%)
  starting transfers between devices  4.6 us (3%)
    psum x1, waiting for transfers between devices, per_device(): summed = lax.psum(attn_terms.astype(jnp.bfloat16), 'tp').astype(jnp.float32)  33.6 us
    unnamed x3, waiting for transfers between devices  21.4 us
    all_gather x1, blocking collectives, per_device(): lax.all_gather(projected[1], 'ctx', axis=0, tiled=True)  17.5 us
    all_gather x1, blocking collectives, per_device(): lax.all_gather(projected[2], 'ctx', axis=0, tiled=True)  16.6 us
    all_to_all x1, blocking collectives, per_device(): lax.all_to_all(activated_part, 'ctx', split_axis=0, concat_axis=1, tiled=...  10.1 us
    all_gather x1, blocking collectives, per_device(): whole_rows = lax.all_gather(frames, 'tp', axis=1, tiled=True)  9.33 us
    convert_element_type x1, other arithmetic, depthwise(): return jax.nn.silu(convolved + bias).astype(jnp.bfloat16)  8.03 us
    unnamed x20, local copies, waits for them, and re-layouts  4.75 us
  transfers between devices with their start and end apart: 3, of which 3 were waited for; matrix products, arithmetic and copies ran while one was open for 3% of the time, Pallas kernels for 0%

commit v1 on v0

--- a/solution.py
+++ b/solution.py
@@ -1,11 +1,18 @@
+import functools
 import math
 
 import jax
 import jax.numpy as jnp
 from jax import lax
+from jax.experimental import pallas as pl
+from jax.experimental.pallas import tpu as pltpu
 from jax.sharding import PartitionSpec as P
 
 HEAD = 96
+HALO = 16
+ROW_CHUNKS = 2
+WINDOW = 256
+MESH = pl.DeviceIdType.MESH
 
 
 def layer_norm(inputs, gain):
@@ -112,6 +119,564 @@
     return (middle.astype(jnp.float32) + conv_sum).astype(jnp.bfloat16)
 
 
+def pick(table, row, column):
+    value = 0
+    for index, line in enumerate(table):
+        value = value + jnp.where(row == index, line[column], 0)
+    return value
+
+
+def norm_rows(parts, gain, store):
+    width = sum(part.shape[-1] for part in parts)
+    total = sum(jnp.sum(part, axis=-1, keepdims=True) for part in parts)
+    average = total / width
+    centered = [part - average for part in parts]
+    squares = sum(jnp.sum(part * part, axis=-1, keepdims=True) for part in centered)
+    scale = lax.rsqrt(squares / width + 1e-05)
+    start = 0
+    for index, part in enumerate(centered):
+        stop = start + part.shape[-1]
+        store(index, (part * scale * gain[:, start:stop]).astype(jnp.bfloat16))
+        start = stop
+
+
+def fused_kernel(
+    ctx_size,
+    tp_size,
+    frames,
+    attn_gain,
+    qkv,
+    out_w,
+    conv_gain,
+    glu_w,
+    depth_k,
+    depth_b,
+    proj_w,
+    out,
+    w_qkv,
+    w_out,
+    w_glu,
+    w_proj,
+    taps,
+    taps32,
+    gathered,
+    normed,
+    q_all,
+    k_all,
+    v_all,
+    context_out,
+    context_in,
+    part32,
+    part16,
+    pair_in,
+    pair_sum,
+    peer_in,
+    middle,
+    glu16,
+    halo_low,
+    halo_high,
+    padded,
+    act,
+    conv32,
+    conv16,
+    conv_pair_in,
+    conv_keep,
+    conv_send,
+    conv_peer_in,
+    local_sem,
+    gather_recv,
+    sib_send,
+    peer_send,
+    up_send,
+    down_send,
+    ctx_send,
+    ctx_recv,
+    stage_send,
+    stage_recv,
+    halo_send,
+    halo_recv,
+):
+    c = lax.axis_index("ctx")
+    t = lax.axis_index("tp")
+    y = t // 2
+    k = t % 2
+    sibling = y * 2 + (1 - k)
+    peer = (1 - y) * 2 + k
+    diagonal = (1 - y) * 2 + (1 - k)
+    rows, cols = frames.shape
+    step_rows = rows // ROW_CHUNKS
+
+    def remote(source, target, send, receive, **device):
+        return pltpu.make_async_remote_copy(
+            src_ref=source,
+            dst_ref=target,
+            send_sem=send,
+            recv_sem=receive,
+            device_id=device,
+            device_id_type=MESH,
+        )
+
+    first_col = c * HEAD
+    window = jnp.minimum(first_col // 128, (cols - WINDOW) // 128)
+    shift = first_col - window * 128
+    window_cols = pl.ds(pl.multiple_of(window * 128, 128), WINDOW)
+
+    def block(ctx_index, tp_index):
+        return gathered.at[tp_index, pl.ds(pl.multiple_of(ctx_index * rows, 16), rows)]
+
+    local = [pltpu.make_async_copy(frames, block(c, t), local_sem.at[0])]
+    for i in range(3):
+        local.append(
+            pltpu.make_async_copy(
+                qkv.at[i, :, window_cols],
+                w_qkv.at[:, pl.ds(i * WINDOW, WINDOW)],
+                local_sem.at[1 + i],
+            )
+        )
+    local.append(pltpu.make_async_copy(out_w, w_out, local_sem.at[4]))
+    for i in range(2):
+        local.append(
+            pltpu.make_async_copy(
+                glu_w.at[i], w_glu.at[:, pl.ds(i * cols, cols)], local_sem.at[5 + i]
+            )
+        )
+    local.append(pltpu.make_async_copy(proj_w, w_proj, local_sem.at[7]))
+    local.append(pltpu.make_async_copy(depth_k, taps, local_sem.at[8]))
+
+    barrier = pltpu.get_barrier_semaphore()
+    for other in (sibling, peer):
+        pl.semaphore_signal(barrier, inc=1, device_id={"tp": other}, device_id_type=MESH)
+    for hop in range(1, ctx_size):
+        pl.semaphore_signal(
+            barrier, inc=1, device_id={"ctx": (c + hop) % ctx_size}, device_id_type=MESH
+        )
+    for copy in local:
+        copy.start()
+    pl.semaphore_wait(barrier, 2 + ctx_size - 1)
+
+    def to_peer(index, source):
+        return remote(source, block(index, t), peer_send.at[index], gather_recv.at[index, t], tp=peer)
+
+    def to_sibling(index, half, source):
+        owner = half * 2 + k
+        return remote(
+            source,
+            block(index, owner),
+            sib_send.at[index, half],
+            gather_recv.at[index, owner],
+            tp=sibling,
+        )
+
+    def up(index, source):
+        return remote(
+            source, block(index, t), up_send.at[index], gather_recv.at[index, t], ctx=c + 1
+        )
+
+    def down(index, source):
+        return remote(
+            source, block(index, t), down_send.at[index], gather_recv.at[index, t], ctx=c - 1
+        )
+
+    def arrived(index, owner):
+        here = block(index, owner)
+        remote(here, here, peer_send.at[index], gather_recv.at[index, owner], tp=peer).wait_recv()
+
+    has_up = c + 1 < ctx_size
+    has_down = c > 0
+
+    pl.when(has_up)(lambda: up(c, frames).start())
+    pl.when(has_down)(lambda: down(c, frames).start())
+    to_peer(c, frames).start()
+    to_sibling(c, y, frames).start()
+
+    order = []
+    for place in range(ctx_size):
+        line = [place]
+        for hop in range(1, ctx_size):
+            line += [i for i in (place - hop, place + hop) if 0 <= i < ctx_size]
+        order.append(line)
+
+    key_lane = lax.broadcasted_iota(jnp.int32, (rows, WINDOW), 1)
+    in_head = (key_lane >= shift) & (key_lane < shift + HEAD)
+    select_row = lax.broadcasted_iota(jnp.int32, (WINDOW, 128), 0)
+    select_col = lax.broadcasted_iota(jnp.int32, (WINDOW, 128), 1)
+    select = ((select_row == select_col + shift) & (select_col < HEAD)).astype(jnp.bfloat16)
+
+    def project(place):
+        index = pick(order, c, place)
+        arrived(index, sibling)
+        arrived(index, diagonal)
+        start = pl.multiple_of(index * rows, 16)
+        sub = rows // 4
+
+        def norm_step(step, carry):
+            at = pl.ds(pl.multiple_of(start + step * sub, 16), sub)
+            to = pl.ds(pl.multiple_of(step * sub, 16), sub)
+
+            def store(part, value):
+                normed[to, part * cols : (part + 1) * cols] = value
+
+            norm_rows(
+                [gathered[i, at, :].astype(jnp.float32) for i in range(tp_size)],
+                attn_gain[...],
+                store,
+            )
+            return carry
+
+        lax.fori_loop(0, 4, norm_step, 0)
+        here = pl.ds(start, rows)
+        projected = jnp.dot(normed[...], w_qkv[...], preferred_element_type=jnp.float32)
+        q_all[here, :] = jnp.where(in_head, projected[:, :WINDOW], 0.0).astype(jnp.bfloat16)
+        k_all[here, :] = projected[:, WINDOW : 2 * WINDOW].astype(jnp.bfloat16)
+        v_all[here, :] = jnp.dot(
+            projected[:, 2 * WINDOW :].astype(jnp.bfloat16),
+            select,
+            preferred_element_type=jnp.float32,
+        ).astype(jnp.bfloat16)
+
+    arrived(c, peer)
+    to_sibling(c, 1 - y, block(c, peer)).start()
+    for hop in range(1, ctx_size):
+
+        @pl.when(c >= hop)
+        def _():
+            index = c - hop
+            arrived(index, t)
+            source = block(index, t)
+            pl.when(has_up)(lambda: up(index, source).start())
+            to_peer(index, source).start()
+            to_sibling(index, y, source).start()
+
+        @pl.when(c + hop < ctx_size)
+        def _():
+            index = c + hop
+            arrived(index, t)
+            source = block(index, t)
+            pl.when(has_down)(lambda: down(index, source).start())
+            to_peer(index, source).start()
+            to_sibling(index, y, source).start()
+
+        if hop == 1:
+            for i in range(4):
+                local[i].wait()
+        project(hop - 1)
+
+        @pl.when(c >= hop)
+        def _():
+            arrived(c - hop, peer)
+            to_sibling(c - hop, 1 - y, block(c - hop, peer)).start()
+
+        @pl.when(c + hop < ctx_size)
+        def _():
+            arrived(c + hop, peer)
+            to_sibling(c + hop, 1 - y, block(c + hop, peer)).start()
+
+    project(ctx_size - 1)
+
+    score_scale = 1.0 / math.sqrt(HEAD)
+
+    def context_copy(index):
+        return remote(
+            context_out.at[index],
+            context_in.at[c],
+            ctx_send.at[index],
+            ctx_recv.at[c],
+            ctx=index,
+        )
+
+    for place in reversed(range(ctx_size)):
+        index = pick(order, c, place)
+        here = pl.ds(pl.multiple_of(index * rows, 16), rows)
+        scores = (
+            lax.dot_general(
+                q_all[here, :],
+                k_all[...],
+                (((1,), (1,)), ((), ())),
+                preferred_element_type=jnp.float32,
+            )
+            * score_scale
+        )
+        weights = jnp.exp(scores - jnp.max(scores, axis=-1, keepdims=True))
+        denominator = jnp.sum(weights, axis=-1, keepdims=True)
+        weighted = jnp.dot(
+            weights.astype(jnp.bfloat16), v_all[...], preferred_element_type=jnp.float32
+        )
+        context = (weighted / denominator).astype(jnp.bfloat16)
+        if place:
+            context_out[index] = context
+            context_copy(index).start()
+        else:
+            context_in[c] = context
+
+    local[4].wait()
+    for hop in range(1, ctx_size):
+        index = (c + hop) % ctx_size
+        remote(
+            context_out.at[index], context_in.at[index], ctx_send.at[index], ctx_recv.at[index], ctx=index
+        ).wait_recv()
+
+    def chunk(step):
+        return pl.ds(step * step_rows, step_rows)
+
+    mine = pl.ds(2 * k, 2)
+    others = pl.ds(2 * (1 - k), 2)
+
+    def stage(kind, step, source, target, device):
+        return remote(
+            source, target, stage_send.at[kind, step], stage_recv.at[kind, step], tp=device
+        )
+
+    def pair_copy(step):
+        return stage(0, step, part16.at[others, chunk(step)], pair_in.at[:, chunk(step)], sibling)
+
+    def peer_copy(step):
+        return stage(1, step, pair_sum.at[:, chunk(step)], peer_in.at[:, chunk(step)], peer)
+
+    def middle_copy(step, half):
+        ref = middle.at[half, chunk(step)]
+        return stage(2, step, ref, ref, sibling)
+
+    for step in range(ROW_CHUNKS):
+        terms = sum(
+            jnp.dot(
+                context_in[head, chunk(step), :HEAD],
+                w_out[head * HEAD : (head + 1) * HEAD, :],
+                preferred_element_type=jnp.float32,
+            )
+            for head in range(ctx_size)
+        )
+        for i in range(tp_size):
+            piece = terms[:, i * cols : (i + 1) * cols]
+            part32[i, chunk(step), :] = piece
+            part16[i, chunk(step), :] = piece.astype(jnp.bfloat16)
+        pair_copy(step).start()
+    for step in range(ROW_CHUNKS):
+        pair_copy(step).wait_recv()
+        pair_sum[:, chunk(step), :] = (
+            part32[mine, chunk(step), :] + pair_in[:, chunk(step), :].astype(jnp.float32)
+        ).astype(jnp.bfloat16)
+        peer_copy(step).start()
+
+    for i in range(5, 9):
+        local[i].wait()
+    taps32[...] = taps[...].astype(jnp.float32)
+
+    def halo_up():
+        return remote(
+            glu16.at[pl.ds(rows - HALO, HALO)], halo_low, halo_send.at[0], halo_recv.at[0], ctx=c + 1
+        )
+
+    def halo_down():
+        return remote(glu16.at[pl.ds(0, HALO)], halo_high, halo_send.at[1], halo_recv.at[1], ctx=c - 1)
+
+    for step in range(ROW_CHUNKS):
+        peer_copy(step).wait_recv()
+        own = pl.ds(pl.multiple_of(c * rows + step * step_rows, 16), step_rows)
+        summed = pair_sum[:, chunk(step), :].astype(jnp.float32) + peer_in[
+            :, chunk(step), :
+        ].astype(jnp.float32)
+        middle[mine, chunk(step), :] = (
+            gathered[mine, own, :].astype(jnp.float32) + summed
+        ).astype(jnp.bfloat16)
+        middle_copy(step, mine).start()
+        middle_copy(step, others).wait_recv()
+
+        def store(part, value):
+            normed[chunk(step), part * cols : (part + 1) * cols] = value
+
+        norm_rows(
+            [middle[i, chunk(step), :].astype(jnp.float32) for i in range(tp_size)],
+            conv_gain[...],
+            store,
+        )
+        halves = jnp.dot(normed[chunk(step), :], w_glu[...], preferred_element_type=jnp.float32)
+        glu = (halves[:, :cols] * jax.nn.sigmoid(halves[:, cols:])).astype(jnp.bfloat16)
+        glu16[chunk(step), :] = glu
+        padded[HALO + step * step_rows : HALO + (step + 1) * step_rows, :] = glu.astype(jnp.float32)
+        if step == 0:
+            pl.when(has_down)(lambda: halo_down().start())
+        if step == ROW_CHUNKS - 1:
+            pl.when(has_up)(lambda: halo_up().start())
+
+    padded[0:HALO, :] = jnp.zeros((HALO, cols), jnp.float32)
+    padded[HALO + rows :, :] = jnp.zeros((HALO, cols), jnp.float32)
+
+    @pl.when(has_down)
+    def _():
+        halo_up().wait_recv()
+        padded[0:HALO, :] = halo_low[...].astype(jnp.float32)
+
+    @pl.when(has_up)
+    def _():
+        halo_down().wait_recv()
+        padded[HALO + rows :, :] = halo_high[...].astype(jnp.float32)
+
+    def conv_pair(step):
+        return stage(
+            3, step, conv16.at[others, chunk(step)], conv_pair_in.at[:, chunk(step)], sibling
+        )
+
+    def conv_peer(step):
+        return stage(4, step, conv_send.at[chunk(step)], conv_peer_in.at[chunk(step)], peer)
+
+    tap_count = taps32.shape[0]
+    first = HALO - tap_count // 2
+    for step in range(ROW_CHUNKS):
+        for lane in range(0, cols, 128):
+            lanes = slice(lane, lane + 128)
+            total = jnp.zeros((step_rows, 128), jnp.float32)
+            for tap in range(tap_count):
+                at = step * step_rows + first + tap
+                total = total + padded[at : at + step_rows, lanes] * taps32[tap : tap + 1, lanes]
+            total = total + depth_b[:, lanes]
+            act[chunk(step), lanes] = (total / (1.0 + jnp.exp(-total))).astype(jnp.bfloat16)
+        terms = jnp.dot(act[chunk(step), :], w_proj[...], preferred_element_type=jnp.float32)
+        for i in range(tp_size):
+            piece = terms[:, i * cols : (i + 1) * cols]
+            slot = (i % 2) * 2 + i // 2
+            conv32[slot, chunk(step), :] = piece
+            conv16[slot, chunk(step), :] = piece.astype(jnp.bfloat16)
+        conv_pair(step).start()
+    for step in range(ROW_CHUNKS):
+        conv_pair(step).wait_recv()
+        conv_send[chunk(step), :] = (
+            conv32[2 * k + 1 - y, chunk(step), :]
+            + conv_pair_in[1 - y, chunk(step), :].astype(jnp.float32)
+        ).astype(jnp.bfloat16)
+        conv_peer(step).start()
+        conv_keep[chunk(step), :] = (
+            conv32[2 * k + y, chunk(step), :]
+            + conv_pair_in[y, chunk(step), :].astype(jnp.float32)
+            + middle[t, chunk(step), :].astype(jnp.float32)
+        )
+    for step in range(ROW_CHUNKS):
+        conv_peer(step).wait_recv()
+        out[chunk(step), :] = (
+            conv_keep[chunk(step), :] + conv_peer_in[chunk(step), :].astype(jnp.float32)
+        ).astype(jnp.bfloat16)
+
+    pl.when(has_up)(lambda: up(c, frames).wait_send())
+    pl.when(has_down)(lambda: down(c, frames).wait_send())
+    to_peer(c, frames).wait_send()
+    to_sibling(c, y, frames).wait_send()
+    to_sibling(c, 1 - y, block(c, peer)).wait_send()
+    for hop in range(1, ctx_size):
+
+        @pl.when(c >= hop)
+        def _():
+            index = c - hop
+            source = block(index, t)
+            pl.when(has_up)(lambda: up(index, source).wait_send())
+            to_peer(index, source).wait_send()
+            to_sibling(index, y, source).wait_send()
+            to_sibling(index, 1 - y, block(index, peer)).wait_send()
+
+        @pl.when(c + hop < ctx_size)
+        def _():
+            index = c + hop
+            source = block(index, t)
+            pl.when(has_down)(lambda: down(index, source).wait_send())
+            to_peer(index, source).wait_send()
+            to_sibling(index, y, source).wait_send()
+            to_sibling(index, 1 - y, block(index, peer)).wait_send()
+
+        context_copy((c + hop) % ctx_size).wait_send()
+    for step in range(ROW_CHUNKS):
+        pair_copy(step).wait_send()
+        peer_copy(step).wait_send()
+        middle_copy(step, mine).wait_send()
+        conv_pair(step).wait_send()
+        conv_peer(step).wait_send()
+    pl.when(has_up)(lambda: halo_up().wait_send())
+    pl.when(has_down)(lambda: halo_down().wait_send())
+
+
+def fused(
+    ctx_size,
+    tp_size,
+    frames,
+    attn_gain,
+    query_key_value,
+    out_weight,
+    conv_gain,
+    glu_weight,
+    depth_kernel,
+    depth_bias,
+    proj_weight,
+):
+    rows, cols = frames.shape
+    width = cols * tp_size
+    all_rows = rows * ctx_size
+    taps = depth_kernel.shape[0]
+    wide, narrow = jnp.float32, jnp.bfloat16
+    vmem = pl.BlockSpec(memory_space=pltpu.VMEM)
+    away = pl.BlockSpec(memory_space=pl.ANY)
+    dma = pltpu.SemaphoreType.DMA
+    return pl.pallas_call(
+        functools.partial(fused_kernel, ctx_size, tp_size),
+        out_shape=jax.ShapeDtypeStruct((rows, cols), narrow),
+        in_specs=[away, vmem, away, away, vmem, away, away, vmem, away],
+        out_specs=vmem,
+        scratch_shapes=[
+            pltpu.VMEM((width, 3 * WINDOW), narrow),
+            pltpu.VMEM((cols, width), narrow),
+            pltpu.VMEM((width, 2 * cols), narrow),
+            pltpu.VMEM((cols, width), narrow),
+            pltpu.VMEM((taps, cols), narrow),
+            pltpu.VMEM((taps, cols), wide),
+            pltpu.VMEM((tp_size, all_rows, cols), narrow),
+            pltpu.VMEM((rows, width), narrow),
+            pltpu.VMEM((all_rows, WINDOW), narrow),
+            pltpu.VMEM((all_rows, WINDOW), narrow),
+            pltpu.VMEM((all_rows, 128), narrow),
+            pltpu.VMEM((ctx_size, rows, 128), narrow),
+            pltpu.VMEM((ctx_size, rows, 128), narrow),
+            pltpu.VMEM((tp_size, rows, cols), wide),
+            pltpu.VMEM((tp_size, rows, cols), narrow),
+            pltpu.VMEM((2, rows, cols), narrow),
+            pltpu.VMEM((2, rows, cols), narrow),
+            pltpu.VMEM((2, rows, cols), narrow),
+            pltpu.VMEM((tp_size, rows, cols), narrow),
+            pltpu.VMEM((rows, cols), narrow),
+            pltpu.VMEM((HALO, cols), narrow),
+            pltpu.VMEM((HALO, cols), narrow),
+            pltpu.VMEM((rows + 2 * HALO, cols), wide),
+            pltpu.VMEM((rows, cols), narrow),
+            pltpu.VMEM((tp_size, rows, cols), wide),
+            pltpu.VMEM((tp_size, rows, cols), narrow),
+            pltpu.VMEM((2, rows, cols), narrow),
+            pltpu.VMEM((rows, cols), wide),
+            pltpu.VMEM((rows, cols), narrow),
+            pltpu.VMEM((rows, cols), narrow),
+            dma((9,)),
+            dma((ctx_size, tp_size)),
+            dma((ctx_size, 2)),
+            dma((ctx_size,)),
+            dma((ctx_size,)),
+            dma((ctx_size,)),
+            dma((ctx_size,)),
+            dma((ctx_size,)),
+            dma((5, ROW_CHUNKS)),
+            dma((5, ROW_CHUNKS)),
+            dma((2,)),
+            dma((2,)),
+        ],
+        compiler_params=pltpu.CompilerParams(
+            collective_id=0, has_side_effects=True, vmem_limit_bytes=48 * 1024 * 1024
+        ),
+    )(
+        frames,
+        attn_gain.reshape(1, -1),
+        query_key_value,
+        out_weight,
+        conv_gain.reshape(1, -1),
+        glu_weight,
+        depth_kernel,
+        depth_bias.reshape(1, -1),
+        proj_weight,
+    )
+
+
 def solution(mesh):
     in_specs = (
         P(("batch", "ctx"), "tp"),
@@ -125,6 +690,14 @@
         P("tp", None),
     )
     out_specs = P(("batch", "ctx"), "tp")
+    ctx_size, tp_size = mesh.shape["ctx"], mesh.shape["tp"]
+
+    def body(frames, attn_gain, query_key_value, *rest):
+        one_head_each = ctx_size * HEAD == query_key_value.shape[2]
+        if tp_size == 4 and one_head_each and frames.shape[0] % (16 * ROW_CHUNKS) == 0:
+            return fused(ctx_size, tp_size, frames, attn_gain, query_key_value, *rest)
+        return per_device(frames, attn_gain, query_key_value, *rest)
+
     return jax.shard_map(
-        per_device, mesh=mesh, in_specs=in_specs, out_specs=out_specs, check_vma=False
+        body, mesh=mesh, in_specs=in_specs, out_specs=out_specs, check_vma=False
     )

time: 180 us -> 61.5 us (0.34)
  waiting for transfers between devices: 57.9 us -> 0 us
  blocking collectives: 53.5 us -> 0 us
  Pallas kernels: 0 us -> 52 us
  other arithmetic: 17 us -> 0 us
  local copies, waits for them, and re-layouts: 22.3 us -> 8.6 us
  between operations: 13.5 us -> 0.02 us
  matrix products: 10 us -> 0 us
  starting transfers between devices: 4.6 us -> 0 us
    pallas_call x0 -> x1, Pallas kernels: none -> 52 us  [fused(): pl.pallas_call(functools.partial(fused_kernel, ctx_size, tp_size), out_sh...]
    all_gather x3 -> x0, blocking collectives: 43.4 us -> none  [the longest x1 17.5 us: per_device(): lax.all_gather(projected[1], 'ctx', axis=0, tiled=True)]
    psum x1 -> x0, waiting for transfers between devices: 33.6 us -> none  [per_device(): summed = lax.psum(attn_terms.astype(jnp.bfloat16), 'tp').astype(jnp.float32)]
    unnamed x3 -> x0, waiting for transfers between devices: 21.4 us -> none
    convert_element_type x3 -> x0, other arithmetic: 10.5 us -> none  [the longest x1 8.03 us: depthwise(): return jax.nn.silu(convolved + bias).astype(jnp.bfloat16)]
    all_to_all x1 -> x0, blocking collectives: 10.1 us -> none  [per_device(): lax.all_to_all(activated_part, 'ctx', split_axis=0, concat_axis=1, tiled=...]
    dot_general x6 -> x0, matrix products: 10 us -> none  [the longest x1 2.66 us: per_device(): jnp.dot(activated, proj_weight, preferred_element_type=jnp.float32)]
    all_to_all x5 -> x0, local copies, waits for them, and re-layouts: 7.86 us -> none  [the longest x3 4.33 us: per_device(): lax.all_to_all(activated_part, 'ctx', split_axis=0, concat_axis=1, tiled=...]
  transfers between devices with their start and end apart: 3 -> 0, of which waited for: 3 -> 0; matrix products, arithmetic and copies ran while one was open for 3% -> 0% of each run, Pallas kernels for 0% -> 0%
where the time goes in v1:
time: 61.5 us; the launch traced here: 60.7 us
  Pallas kernels  52 us (85%)
  local copies, waits for them, and re-layouts  8.6 us (14%)
    pallas_call x1, Pallas kernels, fused(): pl.pallas_call(functools.partial(fused_kernel, ctx_size, tp_size), out_sh...  52 us
    unnamed x11, local copies, waits for them, and re-layouts  6.51 us

profile of v1, /device:TPU:0, one launch (start us, length us, event | category | flops | bytes accessed | tf_op | source)
XLA Modules:
  0.0 60.7 jit_solution(1226061330615475324)
XLA Ops:
  0.0 0.7 %reshape.11.depth_b = f32[1,384]{1,0:T(1,128)S(1)} reshape(f32[384]{0:T(512)} %param.16) | data formatting | bytes 3072 | tf_op jit(solution)/shard_map/reshape | solution.py:675
  0.7 0.7 %reshape.9.attn_gain = f32[1,1536]{1,0:T(1,128)S(1)} reshape(f32[1536]{0:T(1024)} %param.10) | data formatting | bytes 12288 | tf_op jit(solution)/shard_map/reshape | solution.py:669
  1.4 0.7 %reshape.10.conv_gain = f32[1,1536]{1,0:T(1,128)S(1)} reshape(f32[1536]{0:T(1024)} %param.13) | data formatting | bytes 12288 | tf_op jit(solution)/shard_map/reshape | solution.py:672
  2.1 0.0 copy-start
  2.1 1.7 %copy-done = bf16[2,1536,384]{2,1,0:T(8,128)(2,1)S(1)} copy-done((bf16[2,1536,384]{2,1,0:T(8,128)(2,1)S(1)}, bf16[2,1536,384]{2,1,0:T(8,128)(2,1)}, u32[]{:S(2)}) %copy-start) | copy-done | bytes 2359320
  3.8 0.0 copy-start.1
  3.8 1.3 %copy-done.1 = bf16[384,1536]{1,0:T(8,128)(2,1)S(1)} copy-done((bf16[384,1536]{1,0:T(8,128)(2,1)S(1)}, bf16[384,1536]{1,0:T(8,128)(2,1)}, u32[]{:S(2)}) %copy-start.1) | copy-done | bytes 1179672
  5.0 0.0 copy-start.2
  5.0 1.3 %copy-done.2 = bf16[384,1536]{1,0:T(8,128)(2,1)S(1)} copy-done((bf16[384,1536]{1,0:T(8,128)(2,1)S(1)}, bf16[384,1536]{1,0:T(8,128)(2,1)}, u32[]{:S(2)}) %copy-start.2) | copy-done | bytes 1179672
  6.3 0.0 copy-start.3
  6.3 0.9 %copy-done.3 = bf16[192,384]{1,0:T(8,128)(2,1)S(1)} copy-done((bf16[192,384]{1,0:T(8,128)(2,1)S(1)}, bf16[192,384]{1,0:T(8,128)(2,1)}, u32[]{:S(2)}) %copy-start.3) | copy-done | bytes 147480
  7.2 0.0 copy-start.4
  7.2 0.7 %copy-done.4 = bf16[31,384]{1,0:T(8,128)(2,1)S(1)} copy-done((bf16[31,384]{1,0:T(8,128)(2,1)S(1)}, bf16[31,384]{1,0:T(8,128)(2,1)}, u32[]{:S(2)}) %copy-start.4) | copy-done | bytes 23832
  7.9 52.0 %shard_map.91 = bf16[192,384]{1,0:T(8,128)(2,1)S(1)} custom-call(bf16[192,384]{1,0:T(8,128)(2,1)S(1)} %copy-done.3, f32[1,1536]{1,0:T(1,128)S(1)} %reshape.9.attn_gain, bf16[3,1536,384]{2,1,0:T(8,128)(2,1)} %qkv.1, bf16[384,1536]{1,0:T(8,128)(2,1)S(1)} %copy-done.1, f32[1,1536]{1,0:T(1,128)S(1)} %reshape.10.conv_gain, bf16[2,1536,384]{2,1,0:T(8,128)(2,1)S(1)} %copy-done, ...), custom_call_target="tpu_custom_call" | custom-call | tf_op jit(solution)/shard_map/pallas_call | solution.py:615
  60.0 0.7 %copy.11 = bf16[192,384]{1,0:T(8,128)(2,1)} copy(bf16[192,384]{1,0:T(8,128)(2,1)S(1)} %shard_map.91) | data formatting | bytes 294912
Async XLA Ops:
  2.1 1.7 %copy-start = (bf16[2,1536,384]{2,1,0:T(8,128)(2,1)S(1)}, bf16[2,1536,384]{2,1,0:T(8,128)(2,1)}, u32[]{:S(2)}) copy-start(bf16[2,1536,384]{2,1,0:T(8,128)(2,1)} %glu_w.1) | copy-start | bytes 7077892
  3.8 1.3 %copy-start.1 = (bf16[384,1536]{1,0:T(8,128)(2,1)S(1)}, bf16[384,1536]{1,0:T(8,128)(2,1)}, u32[]{:S(2)}) copy-start(bf16[384,1536]{1,0:T(8,128)(2,1)} %out_w.1) | copy-start | bytes 3538948
  5.0 1.3 %copy-start.2 = (bf16[384,1536]{1,0:T(8,128)(2,1)S(1)}, bf16[384,1536]{1,0:T(8,128)(2,1)}, u32[]{:S(2)}) copy-start(bf16[384,1536]{1,0:T(8,128)(2,1)} %proj_w.1) | copy-start | bytes 3538948
  6.3 0.9 %copy-start.3 = (bf16[192,384]{1,0:T(8,128)(2,1)S(1)}, bf16[192,384]{1,0:T(8,128)(2,1)}, u32[]{:S(2)}) copy-start(bf16[192,384]{1,0:T(8,128)(2,1)} %frames.1) | copy-start | bytes 442372
  7.2 0.7 %copy-start.4 = (bf16[31,384]{1,0:T(8,128)(2,1)S(1)}, bf16[31,384]{1,0:T(8,128)(2,1)}, u32[]{:S(2)}) copy-start(bf16[31,384]{1,0:T(8,128)(2,1)} %depth_k.1) | copy-start | bytes 71428

commit v2 on v1

--- a/solution.py
+++ b/solution.py
@@ -11,6 +11,7 @@
 HEAD = 96
 HALO = 16
 ROW_CHUNKS = 2
+PARTS = 2
 WINDOW = 256
 MESH = pl.DeviceIdType.MESH
 
@@ -159,6 +160,9 @@
     w_proj,
     taps,
     taps32,
+    attn_scale,
+    conv_scale,
+    bias,
     gathered,
     normed,
     q_all,
@@ -221,8 +225,14 @@
     shift = first_col - window * 128
     window_cols = pl.ds(pl.multiple_of(window * 128, 128), WINDOW)
 
-    def block(ctx_index, tp_index):
-        return gathered.at[tp_index, pl.ds(pl.multiple_of(ctx_index * rows, 16), rows)]
+    part_rows = rows // PARTS
+
+    def block(ctx_index, tp_index, part=None):
+        if part is None:
+            at = pl.ds(pl.multiple_of(ctx_index * rows, 16), rows)
+        else:
+            at = pl.ds(pl.multiple_of(ctx_index * rows + part * part_rows, 16), part_rows)
+        return gathered.at[tp_index, at]
 
     local = [pltpu.make_async_copy(frames, block(c, t), local_sem.at[0])]
     for i in range(3):
@@ -242,6 +252,9 @@
         )
     local.append(pltpu.make_async_copy(proj_w, w_proj, local_sem.at[7]))
     local.append(pltpu.make_async_copy(depth_k, taps, local_sem.at[8]))
+    local.append(pltpu.make_async_copy(conv_gain, conv_scale, local_sem.at[9]))
+    local.append(pltpu.make_async_copy(depth_b, bias, local_sem.at[10]))
+    local.insert(4, pltpu.make_async_copy(attn_gain, attn_scale, local_sem.at[11]))
 
     barrier = pltpu.get_barrier_semaphore()
     for other in (sibling, peer):
@@ -254,40 +267,61 @@
         copy.start()
     pl.semaphore_wait(barrier, 2 + ctx_size - 1)
 
-    def to_peer(index, source):
-        return remote(source, block(index, t), peer_send.at[index], gather_recv.at[index, t], tp=peer)
-
-    def to_sibling(index, half, source):
+    def own_part(part):
+        return frames.at[pl.ds(part * part_rows, part_rows)]
+
+    def to_peer(index, part, source):
+        return remote(
+            source,
+            block(index, t, part),
+            peer_send.at[index, part],
+            gather_recv.at[index, t, part],
+            tp=peer,
+        )
+
+    def to_sibling(index, half, part, source):
         owner = half * 2 + k
         return remote(
             source,
-            block(index, owner),
-            sib_send.at[index, half],
-            gather_recv.at[index, owner],
+            block(index, owner, part),
+            sib_send.at[index, half, part],
+            gather_recv.at[index, owner, part],
             tp=sibling,
         )
 
-    def up(index, source):
+    def up(index, part, source):
         return remote(
-            source, block(index, t), up_send.at[index], gather_recv.at[index, t], ctx=c + 1
-        )
-
-    def down(index, source):
+            source,
+            block(index, t, part),
+            up_send.at[index, part],
+            gather_recv.at[index, t, part],
+            ctx=c + 1,
+        )
+
+    def down(index, part, source):
         return remote(
-            source, block(index, t), down_send.at[index], gather_recv.at[index, t], ctx=c - 1
-        )
-
-    def arrived(index, owner):
-        here = block(index, owner)
-        remote(here, here, peer_send.at[index], gather_recv.at[index, owner], tp=peer).wait_recv()
+            source,
+            block(index, t, part),
+            down_send.at[index, part],
+            gather_recv.at[index, t, part],
+            ctx=c - 1,
+        )
+
+    def arrived(index, owner, part):
+        here = block(index, owner, part)
+        remote(
+            here, here, peer_send.at[index, part], gather_recv.at[index, owner, part], tp=peer
+        ).wait_recv()
 
     has_up = c + 1 < ctx_size
     has_down = c > 0
 
-    pl.when(has_up)(lambda: up(c, frames).start())
-    pl.when(has_down)(lambda: down(c, frames).start())
-    to_peer(c, frames).start()
-    to_sibling(c, y, frames).start()
+    for part in range(PARTS):
+        source = own_part(part)
+        pl.when(has_up)(lambda: up(c, part, source).start())
+        pl.when(has_down)(lambda: down(c, part, source).start())
+        to_peer(c, part, source).start()
+        to_sibling(c, y, part, source).start()
 
     order = []
     for place in range(ctx_size):
@@ -304,8 +338,9 @@
 
     def project(place):
         index = pick(order, c, place)
-        arrived(index, sibling)
-        arrived(index, diagonal)
+        for part in range(PARTS):
+            arrived(index, sibling, part)
+            arrived(index, diagonal, part)
         start = pl.multiple_of(index * rows, 16)
         sub = rows // 4
 
@@ -318,7 +353,7 @@
 
             norm_rows(
                 [gathered[i, at, :].astype(jnp.float32) for i in range(tp_size)],
-                attn_gain[...],
+                attn_scale[...].reshape(1, -1),
                 store,
             )
             return carry
@@ -334,43 +369,49 @@
             preferred_element_type=jnp.float32,
         ).astype(jnp.bfloat16)
 
-    arrived(c, peer)
-    to_sibling(c, 1 - y, block(c, peer)).start()
-    for hop in range(1, ctx_size):
-
-        @pl.when(c >= hop)
-        def _():
-            index = c - hop
-            arrived(index, t)
-            source = block(index, t)
-            pl.when(has_up)(lambda: up(index, source).start())
-            to_peer(index, source).start()
-            to_sibling(index, y, source).start()
-
-        @pl.when(c + hop < ctx_size)
-        def _():
-            index = c + hop
-            arrived(index, t)
-            source = block(index, t)
-            pl.when(has_down)(lambda: down(index, source).start())
-            to_peer(index, source).start()
-            to_sibling(index, y, source).start()
-
-        if hop == 1:
-            for i in range(4):
-                local[i].wait()
-        project(hop - 1)
-
-        @pl.when(c >= hop)
-        def _():
-            arrived(c - hop, peer)
-            to_sibling(c - hop, 1 - y, block(c - hop, peer)).start()
-
-        @pl.when(c + hop < ctx_size)
-        def _():
-            arrived(c + hop, peer)
-            to_sibling(c + hop, 1 - y, block(c + hop, peer)).start()
-
+    def pass_on(hop):
+        for part in range(PARTS):
+
+            @pl.when(c >= hop)
+            def _():
+                index = c - hop
+                arrived(index, t, part)
+                source = block(index, t, part)
+                pl.when(has_up)(lambda: up(index, part, source).start())
+                to_peer(index, part, source).start()
+                to_sibling(index, y, part, source).start()
+
+            @pl.when(c + hop < ctx_size)
+            def _():
+                index = c + hop
+                arrived(index, t, part)
+                source = block(index, t, part)
+                pl.when(has_down)(lambda: down(index, part, source).start())
+                to_peer(index, part, source).start()
+                to_sibling(index, y, part, source).start()
+
+    def from_peer(place):
+        index = pick(order, c, place)
+        for part in range(PARTS):
+            arrived(index, peer, part)
+            to_sibling(index, 1 - y, part, block(index, peer, part)).start()
+
+    pass_on(1)
+    from_peer(0)
+    pass_on(2)
+    from_peer(1)
+    for i in range(5):
+        local[i].wait()
+    project(0)
+    for place in range(2, ctx_size):
+        last = place == ctx_size - 1
+        if not last:
+            pass_on(place + 1)
+        else:
+            project(place - 1)
+        from_peer(place)
+        if not last:
+            project(place - 1)
     project(ctx_size - 1)
 
     score_scale = 1.0 / math.sqrt(HEAD)
@@ -408,7 +449,7 @@
         else:
             context_in[c] = context
 
-    local[4].wait()
+    local[5].wait()
     for hop in range(1, ctx_size):
         index = (c + hop) % ctx_size
         remote(
@@ -457,7 +498,7 @@
         ).astype(jnp.bfloat16)
         peer_copy(step).start()
 
-    for i in range(5, 9):
+    for i in range(6, 12):
         local[i].wait()
     taps32[...] = taps[...].astype(jnp.float32)
 
@@ -486,7 +527,7 @@
 
         norm_rows(
             [middle[i, chunk(step), :].astype(jnp.float32) for i in range(tp_size)],
-            conv_gain[...],
+            conv_scale[...].reshape(1, -1),
             store,
         )
         halves = jnp.dot(normed[chunk(step), :], w_glu[...], preferred_element_type=jnp.float32)
@@ -528,7 +569,7 @@
             for tap in range(tap_count):
                 at = step * step_rows + first + tap
                 total = total + padded[at : at + step_rows, lanes] * taps32[tap : tap + 1, lanes]
-            total = total + depth_b[:, lanes]
+            total = total + bias[lanes].reshape(1, -1)
             act[chunk(step), lanes] = (total / (1.0 + jnp.exp(-total))).astype(jnp.bfloat16)
         terms = jnp.dot(act[chunk(step), :], w_proj[...], preferred_element_type=jnp.float32)
         for i in range(tp_size):
@@ -555,31 +596,16 @@
             conv_keep[chunk(step), :] + conv_peer_in[chunk(step), :].astype(jnp.float32)
         ).astype(jnp.bfloat16)
 
-    pl.when(has_up)(lambda: up(c, frames).wait_send())
-    pl.when(has_down)(lambda: down(c, frames).wait_send())
-    to_peer(c, frames).wait_send()
-    to_sibling(c, y, frames).wait_send()
-    to_sibling(c, 1 - y, block(c, peer)).wait_send()
+    for place in range(ctx_size):
+        for part in range(PARTS):
+            index = pick(order, c, place)
+            source = block(index, t, part)
+            pl.when(has_up & (index <= c))(lambda: up(index, part, source).wait_send())
+            pl.when(has_down & (index >= c))(lambda: down(index, part, source).wait_send())
+            to_peer(index, part, source).wait_send()
+            to_sibling(index, y, part, source).wait_send()
+            to_sibling(index, 1 - y, part, source).wait_send()
     for hop in range(1, ctx_size):
-
-        @pl.when(c >= hop)
-        def _():
-            index = c - hop
-            source = block(index, t)
-            pl.when(has_up)(lambda: up(index, source).wait_send())
-            to_peer(index, source).wait_send()
-            to_sibling(index, y, source).wait_send()
-            to_sibling(index, 1 - y, block(index, peer)).wait_send()
-
-        @pl.when(c + hop < ctx_size)
-        def _():
-            index = c + hop
-            source = block(index, t)
-            pl.when(has_down)(lambda: down(index, source).wait_send())
-            to_peer(index, source).wait_send()
-            to_sibling(index, y, source).wait_send()
-            to_sibling(index, 1 - y, block(index, peer)).wait_send()
-
         context_copy((c + hop) % ctx_size).wait_send()
     for step in range(ROW_CHUNKS):
         pair_copy(step).wait_send()
@@ -610,12 +636,12 @@
     taps = depth_kernel.shape[0]
     wide, narrow = jnp.float32, jnp.bfloat16
     vmem = pl.BlockSpec(memory_space=pltpu.VMEM)
-    away = pl.BlockSpec(memory_space=pl.ANY)
+    away = pl.BlockSpec(memory_space=pltpu.HBM)
     dma = pltpu.SemaphoreType.DMA
     return pl.pallas_call(
         functools.partial(fused_kernel, ctx_size, tp_size),
         out_shape=jax.ShapeDtypeStruct((rows, cols), narrow),
-        in_specs=[away, vmem, away, away, vmem, away, away, vmem, away],
+        in_specs=[away] * 9,
         out_specs=vmem,
         scratch_shapes=[
             pltpu.VMEM((width, 3 * WINDOW), narrow),
@@ -624,6 +650,9 @@
             pltpu.VMEM((cols, width), narrow),
             pltpu.VMEM((taps, cols), narrow),
             pltpu.VMEM((taps, cols), wide),
+            pltpu.VMEM((width,), wide),
+            pltpu.VMEM((width,), wide),
+            pltpu.VMEM((cols,), wide),
             pltpu.VMEM((tp_size, all_rows, cols), narrow),
             pltpu.VMEM((rows, width), narrow),
             pltpu.VMEM((all_rows, WINDOW), narrow),
@@ -648,12 +677,12 @@
             pltpu.VMEM((rows, cols), wide),
             pltpu.VMEM((rows, cols), narrow),
             pltpu.VMEM((rows, cols), narrow),
-            dma((9,)),
-            dma((ctx_size, tp_size)),
-            dma((ctx_size, 2)),
-            dma((ctx_size,)),
-            dma((ctx_size,)),
-            dma((ctx_size,)),
+            dma((12,)),
+            dma((ctx_size, tp_size, PARTS)),
+            dma((ctx_size, 2, PARTS)),
+            dma((ctx_size, PARTS)),
+            dma((ctx_size, PARTS)),
+            dma((ctx_size, PARTS)),
             dma((ctx_size,)),
             dma((ctx_size,)),
             dma((5, ROW_CHUNKS)),
@@ -662,17 +691,17 @@
             dma((2,)),
         ],
         compiler_params=pltpu.CompilerParams(
-            collective_id=0, has_side_effects=True, vmem_limit_bytes=48 * 1024 * 1024
+            collective_id=0, has_side_effects=True, vmem_limit_bytes=62 * 1024 * 1024
         ),
     )(
         frames,
-        attn_gain.reshape(1, -1),
+        attn_gain,
         query_key_value,
         out_weight,
-        conv_gain.reshape(1, -1),
+        conv_gain,
         glu_weight,
         depth_kernel,
-        depth_bias.reshape(1, -1),
+        depth_bias,
         proj_weight,
     )
 
@@ -694,7 +723,8 @@
 
     def body(frames, attn_gain, query_key_value, *rest):
         one_head_each = ctx_size * HEAD == query_key_value.shape[2]
-        if tp_size == 4 and one_head_each and frames.shape[0] % (16 * ROW_CHUNKS) == 0:
+        even = frames.shape[0] % (16 * ROW_CHUNKS * PARTS) == 0
+        if tp_size == 4 and one_head_each and ctx_size > 2 and even:
             return fused(ctx_size, tp_size, frames, attn_gain, query_key_value, *rest)
         return per_device(frames, attn_gain, query_key_value, *rest)
 

time: 61.5 us -> 54.3 us (0.88)
  local copies, waits for them, and re-layouts: 8.6 us -> 1.59 us
    unnamed x11 -> x1, local copies, waits for them, and re-layouts: 6.51 us -> 1.59 us
    reshape x3 -> x0, local copies, waits for them, and re-layouts: 2.08 us -> none  [the longest x1 0.7 us: fused(): attn_gain.reshape(1, -1)]
where the time goes in v2:
time: 54.3 us; the launch traced here: 53.7 us
  Pallas kernels  52.1 us (96%)
  local copies, waits for them, and re-layouts  1.59 us (3%)
    pallas_call x1, Pallas kernels, fused(): pl.pallas_call(functools.partial(fused_kernel, ctx_size, tp_size), out_sh...  52.1 us
    unnamed x1, local copies, waits for them, and re-layouts  1.59 us

profile of v2, /device:TPU:0, one launch (start us, length us, event | category | flops | bytes accessed | tf_op | source)
XLA Modules:
  0.0 53.7 jit_solution(16785262810736352158)
XLA Ops:
  0.0 52.1 %shard_map.91 = bf16[192,384]{1,0:T(8,128)(2,1)} custom-call(bf16[192,384]{1,0:T(8,128)(2,1)} %frames.1, f32[1536]{0:T(1024)} %attn_gain.1, bf16[3,1536,384]{2,1,0:T(8,128)(2,1)} %qkv.1, bf16[384,1536]{1,0:T(8,128)(2,1)} %out_w.1, f32[1536]{0:T(1024)} %conv_gain.1, bf16[2,1536,384]{2,1,0:T(8,128)(2,1)} %glu_w.1, bf16[31,384]{1,0:T(8,128)(2,1)} %depth_k.1, ...), custom_call_target="tpu_custom_call" | custom-call | tf_op jit(solution)/shard_map/pallas_call | solution.py:641
  52.1 1.6 %copy.11 = bf16[192,384]{1,0:T(8,128)(2,1)} copy(bf16[192,384]{1,0:T(8,128)(2,1)} %shard_map.91) | data formatting | bytes 294912

commit v3 on v2

--- a/solution.py
+++ b/solution.py
@@ -338,27 +338,22 @@
 
     def project(place):
         index = pick(order, c, place)
+        start = pl.multiple_of(index * rows, 16)
+        sub = part_rows // 2
         for part in range(PARTS):
             arrived(index, sibling, part)
             arrived(index, diagonal, part)
-        start = pl.multiple_of(index * rows, 16)
-        sub = rows // 4
-
-        def norm_step(step, carry):
-            at = pl.ds(pl.multiple_of(start + step * sub, 16), sub)
-            to = pl.ds(pl.multiple_of(step * sub, 16), sub)
-
-            def store(part, value):
-                normed[to, part * cols : (part + 1) * cols] = value
-
-            norm_rows(
-                [gathered[i, at, :].astype(jnp.float32) for i in range(tp_size)],
-                attn_scale[...].reshape(1, -1),
-                store,
-            )
-            return carry
-
-        lax.fori_loop(0, 4, norm_step, 0)
+            for step in range(2 * part, 2 * part + 2):
+                at = pl.ds(pl.multiple_of(start + step * sub, 16), sub)
+
+                def store(piece, value):
+                    normed[pl.ds(step * sub, sub), piece * cols : (piece + 1) * cols] = value
+
+                norm_rows(
+                    [gathered[i, at, :].astype(jnp.float32) for i in range(tp_size)],
+                    attn_scale[...].reshape(1, -1),
+                    store,
+                )
         here = pl.ds(start, rows)
         projected = jnp.dot(normed[...], w_qkv[...], preferred_element_type=jnp.float32)
         q_all[here, :] = jnp.where(in_head, projected[:, :WINDOW], 0.0).astype(jnp.bfloat16)
@@ -416,18 +411,21 @@
 
     score_scale = 1.0 / math.sqrt(HEAD)
 
-    def context_copy(index):
+    def chunk(step):
+        return pl.ds(step * step_rows, step_rows)
+
+    def context_copy(index, step):
         return remote(
-            context_out.at[index],
-            context_in.at[c],
-            ctx_send.at[index],
-            ctx_recv.at[c],
+            context_out.at[index, chunk(step)],
+            context_in.at[c, chunk(step)],
+            ctx_send.at[index, step],
+            ctx_recv.at[c, step],
             ctx=index,
         )
 
-    for place in reversed(range(ctx_size)):
+    def attend(step, place):
         index = pick(order, c, place)
-        here = pl.ds(pl.multiple_of(index * rows, 16), rows)
+        here = pl.ds(pl.multiple_of(index * rows + step * step_rows, 16), step_rows)
         scores = (
             lax.dot_general(
                 q_all[here, :],
@@ -444,20 +442,15 @@
         )
         context = (weighted / denominator).astype(jnp.bfloat16)
         if place:
-            context_out[index] = context
-            context_copy(index).start()
+            context_out[index, chunk(step), :] = context
+            context_copy(index, step).start()
         else:
-            context_in[c] = context
-
+            context_in[c, chunk(step), :] = context
+
+    for step in range(ROW_CHUNKS):
+        for place in reversed(range(ctx_size)):
+            attend(step, place)
     local[5].wait()
-    for hop in range(1, ctx_size):
-        index = (c + hop) % ctx_size
-        remote(
-            context_out.at[index], context_in.at[index], ctx_send.at[index], ctx_recv.at[index], ctx=index
-        ).wait_recv()
-
-    def chunk(step):
-        return pl.ds(step * step_rows, step_rows)
 
     mine = pl.ds(2 * k, 2)
     others = pl.ds(2 * (1 - k), 2)
@@ -478,6 +471,10 @@
         return stage(2, step, ref, ref, sibling)
 
     for step in range(ROW_CHUNKS):
+        for hop in range(1, ctx_size):
+            index = (c + hop) % ctx_size
+            here = context_in.at[index, chunk(step)]
+            remote(here, here, ctx_send.at[index, step], ctx_recv.at[index, step], ctx=index).wait_recv()
         terms = sum(
             jnp.dot(
                 context_in[head, chunk(step), :HEAD],
@@ -539,18 +536,21 @@
         if step == ROW_CHUNKS - 1:
             pl.when(has_up)(lambda: halo_up().start())
 
-    padded[0:HALO, :] = jnp.zeros((HALO, cols), jnp.float32)
-    padded[HALO + rows :, :] = jnp.zeros((HALO, cols), jnp.float32)
-
-    @pl.when(has_down)
-    def _():
-        halo_up().wait_recv()
-        padded[0:HALO, :] = halo_low[...].astype(jnp.float32)
-
-    @pl.when(has_up)
-    def _():
-        halo_down().wait_recv()
-        padded[HALO + rows :, :] = halo_high[...].astype(jnp.float32)
+    def edge_low():
+        padded[0:HALO, :] = jnp.zeros((HALO, cols), jnp.float32)
+
+        @pl.when(has_down)
+        def _():
+            halo_up().wait_recv()
+            padded[0:HALO, :] = halo_low[...].astype(jnp.float32)
+
+    def edge_high():
+        padded[HALO + rows :, :] = jnp.zeros((HALO, cols), jnp.float32)
+
+        @pl.when(has_up)
+        def _():
+            halo_down().wait_recv()
+            padded[HALO + rows :, :] = halo_high[...].astype(jnp.float32)
 
     def conv_pair(step):
         return stage(
@@ -562,7 +562,12 @@
 
     tap_count = taps32.shape[0]
     first = HALO - tap_count // 2
-    for step in range(ROW_CHUNKS):
+    last_first = list(reversed(range(ROW_CHUNKS)))
+    for step in last_first:
+        if step == ROW_CHUNKS - 1:
+            edge_high()
+        if step == 0:
+            edge_low()
         for lane in range(0, cols, 128):
             lanes = slice(lane, lane + 128)
             total = jnp.zeros((step_rows, 128), jnp.float32)
@@ -578,7 +583,7 @@
             conv32[slot, chunk(step), :] = piece
             conv16[slot, chunk(step), :] = piece.astype(jnp.bfloat16)
         conv_pair(step).start()
-    for step in range(ROW_CHUNKS):
+    for step in last_first:
         conv_pair(step).wait_recv()
         conv_send[chunk(step), :] = (
             conv32[2 * k + 1 - y, chunk(step), :]
@@ -590,7 +595,7 @@
             + conv_pair_in[y, chunk(step), :].astype(jnp.float32)
             + middle[t, chunk(step), :].astype(jnp.float32)
         )
-    for step in range(ROW_CHUNKS):
+    for step in last_first:
         conv_peer(step).wait_recv()
         out[chunk(step), :] = (
             conv_keep[chunk(step), :] + conv_peer_in[chunk(step), :].astype(jnp.float32)
@@ -606,7 +611,8 @@
             to_sibling(index, y, part, source).wait_send()
             to_sibling(index, 1 - y, part, source).wait_send()
     for hop in range(1, ctx_size):
-        context_copy((c + hop) % ctx_size).wait_send()
+        for step in range(ROW_CHUNKS):
+            context_copy((c + hop) % ctx_size, step).wait_send()
     for step in range(ROW_CHUNKS):
         pair_copy(step).wait_send()
         peer_copy(step).wait_send()
@@ -683,8 +689,8 @@
             dma((ctx_size, PARTS)),
             dma((ctx_size, PARTS)),
             dma((ctx_size, PARTS)),
-            dma((ctx_size,)),
-            dma((ctx_size,)),
+            dma((ctx_size, ROW_CHUNKS)),
+            dma((ctx_size, ROW_CHUNKS)),
             dma((5, ROW_CHUNKS)),
             dma((5, ROW_CHUNKS)),
             dma((2,)),

time: 54.3 us -> 51.8 us (0.954)
  Pallas kernels: 52.1 us -> 50.1 us
    pallas_call x1, Pallas kernels: 52.1 us -> 50.1 us  [fused(): pl.pallas_call(functools.partial(fused_kernel, ctx_size, tp_size), out_sh...]
where the time goes in v3:
time: 51.8 us; the launch traced here: 51.7 us
  Pallas kernels  50.1 us (97%)
  local copies, waits for them, and re-layouts  1.59 us (3%)
    pallas_call x1, Pallas kernels, fused(): pl.pallas_call(functools.partial(fused_kernel, ctx_size, tp_size), out_sh...  50.1 us
    unnamed x1, local copies, waits for them, and re-layouts  1.59 us

profile of v3, /device:TPU:0, one launch (start us, length us, event | category | flops | bytes accessed | tf_op | source)
XLA Modules:
  0.0 51.7 jit_solution(5467031161319960794)
XLA Ops:
  0.0 50.1 %shard_map.91 = bf16[192,384]{1,0:T(8,128)(2,1)} custom-call(bf16[192,384]{1,0:T(8,128)(2,1)} %frames.1, f32[1536]{0:T(1024)} %attn_gain.1, bf16[3,1536,384]{2,1,0:T(8,128)(2,1)} %qkv.1, bf16[384,1536]{1,0:T(8,128)(2,1)} %out_w.1, f32[1536]{0:T(1024)} %conv_gain.1, bf16[2,1536,384]{2,1,0:T(8,128)(2,1)} %glu_w.1, bf16[31,384]{1,0:T(8,128)(2,1)} %depth_k.1, ...), custom_call_target="tpu_custom_call" | custom-call | tf_op jit(solution)/shard_map/pallas_call | solution.py:647
  50.1 1.6 %copy.11 = bf16[192,384]{1,0:T(8,128)(2,1)} copy(bf16[192,384]{1,0:T(8,128)(2,1)} %shard_map.91) | data formatting | bytes 294912

commit v4 on v3

--- a/solution.py
+++ b/solution.py
@@ -10,7 +10,7 @@
 
 HEAD = 96
 HALO = 16
-ROW_CHUNKS = 2
+ROW_CHUNKS = 3
 PARTS = 2
 WINDOW = 256
 MESH = pl.DeviceIdType.MESH

time: 51.8 us -> 53.6 us (1.035)
  Pallas kernels: 50.1 us -> 51.9 us
    pallas_call x1, Pallas kernels: 50.1 us -> 51.9 us  [fused(): pl.pallas_call(functools.partial(fused_kernel, ctx_size, tp_size), out_sh...]
where the time goes in v4:
time: 53.6 us; the launch traced here: 53.5 us
  Pallas kernels  51.9 us (97%)
  local copies, waits for them, and re-layouts  1.59 us (3%)
    pallas_call x1, Pallas kernels, fused(): pl.pallas_call(functools.partial(fused_kernel, ctx_size, tp_size), out_sh...  51.9 us
    unnamed x1, local copies, waits for them, and re-layouts  1.59 us

profile of v4, /device:TPU:0, one launch (start us, length us, event | category | flops | bytes accessed | tf_op | source)
XLA Modules:
  0.0 53.5 jit_solution(2629267831802344734)
XLA Ops:
  0.0 51.9 %shard_map.91 = bf16[192,384]{1,0:T(8,128)(2,1)} custom-call(bf16[192,384]{1,0:T(8,128)(2,1)} %frames.1, f32[1536]{0:T(1024)} %attn_gain.1, bf16[3,1536,384]{2,1,0:T(8,128)(2,1)} %qkv.1, bf16[384,1536]{1,0:T(8,128)(2,1)} %out_w.1, f32[1536]{0:T(1024)} %conv_gain.1, bf16[2,1536,384]{2,1,0:T(8,128)(2,1)} %glu_w.1, bf16[31,384]{1,0:T(8,128)(2,1)} %depth_k.1, ...), custom_call_target="tpu_custom_call" | custom-call | tf_op jit(solution)/shard_map/pallas_call | solution.py:647
  51.9 1.6 %copy.11 = bf16[192,384]{1,0:T(8,128)(2,1)} copy(bf16[192,384]{1,0:T(8,128)(2,1)} %shard_map.91) | data formatting | bytes 294912

commit v5 on v3

--- a/solution.py
+++ b/solution.py
@@ -193,6 +193,7 @@
     peer_send,
     up_send,
     down_send,
+    side_send,
     ctx_send,
     ctx_recv,
     stage_send,
@@ -307,6 +308,17 @@
             ctx=c - 1,
         )
 
+    end = ctx_size - 1
+    late = PARTS - 1
+
+    def side_up():
+        here = block(0, peer, late)
+        return remote(here, here, side_send.at[0], gather_recv.at[0, peer, late], ctx=c + 1)
+
+    def side_down():
+        here = block(end, peer, late)
+        return remote(here, here, side_send.at[1], gather_recv.at[end, peer, late], ctx=c - 1)
+
     def arrived(index, owner, part):
         here = block(index, owner, part)
         remote(
@@ -373,7 +385,10 @@
                 arrived(index, t, part)
                 source = block(index, t, part)
                 pl.when(has_up)(lambda: up(index, part, source).start())
-                to_peer(index, part, source).start()
+                if part == late:
+                    pl.when(index > 0)(lambda: to_peer(index, part, source).start())
+                else:
+                    to_peer(index, part, source).start()
                 to_sibling(index, y, part, source).start()
 
             @pl.when(c + hop < ctx_size)
@@ -382,18 +397,45 @@
                 arrived(index, t, part)
                 source = block(index, t, part)
                 pl.when(has_down)(lambda: down(index, part, source).start())
-                to_peer(index, part, source).start()
+                if part == late:
+                    pl.when(index < end)(lambda: to_peer(index, part, source).start())
+                else:
+                    to_peer(index, part, source).start()
                 to_sibling(index, y, part, source).start()
+
+    def pass_side(hop):
+        @pl.when(c == hop)
+        def _():
+            arrived(0, peer, late)
+            pl.when(has_up)(lambda: side_up().start())
+            to_sibling(0, 1 - y, late, block(0, peer, late)).start()
+
+        @pl.when(c + hop == end)
+        def _():
+            arrived(end, peer, late)
+            pl.when(has_down)(lambda: side_down().start())
+            to_sibling(end, 1 - y, late, block(end, peer, late)).start()
 
     def from_peer(place):
         index = pick(order, c, place)
-        for part in range(PARTS):
+
+        def take(part):
             arrived(index, peer, part)
             to_sibling(index, 1 - y, part, block(index, peer, part)).start()
+
+        for part in range(PARTS):
+            if part == late and place:
+                pl.when((index > 0) & (index < end))(lambda: take(part))
+            else:
+                take(part)
+        if not place:
+            pl.when(c == 0)(lambda: side_up().start())
+            pl.when(c == end)(lambda: side_down().start())
 
     pass_on(1)
     from_peer(0)
     pass_on(2)
+    pass_side(1)
     from_peer(1)
     for i in range(5):
         local[i].wait()
@@ -404,6 +446,7 @@
             pass_on(place + 1)
         else:
             project(place - 1)
+        pass_side(place)
         from_peer(place)
         if not last:
             project(place - 1)
@@ -607,9 +650,15 @@
             source = block(index, t, part)
             pl.when(has_up & (index <= c))(lambda: up(index, part, source).wait_send())
             pl.when(has_down & (index >= c))(lambda: down(index, part, source).wait_send())
-            to_peer(index, part, source).wait_send()
+            if part == late:
+                crossed = (index == c) | ((index > 0) & (index < end))
+                pl.when(crossed)(lambda: to_peer(index, part, source).wait_send())
+            else:
+                to_peer(index, part, source).wait_send()
             to_sibling(index, y, part, source).wait_send()
             to_sibling(index, 1 - y, part, source).wait_send()
+    pl.when(has_up)(lambda: side_up().wait_send())
+    pl.when(has_down)(lambda: side_down().wait_send())
     for hop in range(1, ctx_size):
         for step in range(ROW_CHUNKS):
             context_copy((c + hop) % ctx_size, step).wait_send()
@@ -689,6 +738,7 @@
             dma((ctx_size, PARTS)),
             dma((ctx_size, PARTS)),
             dma((ctx_size, PARTS)),
+            dma((2,)),
             dma((ctx_size, ROW_CHUNKS)),
             dma((ctx_size, ROW_CHUNKS)),
             dma((5, ROW_CHUNKS)),

time: 51.8 us -> 51.8 us (level)
  no operation moved by 1% of the time
where the time goes in v5:
time: 51.8 us; the launch traced here: 51.7 us
  Pallas kernels  50.1 us (97%)
  local copies, waits for them, and re-layouts  1.59 us (3%)
    pallas_call x1, Pallas kernels, fused(): pl.pallas_call(functools.partial(fused_kernel, ctx_size, tp_size), out_sh...  50.1 us
    unnamed x1, local copies, waits for them, and re-layouts  1.59 us

profile of v5, /device:TPU:0, one launch (start us, length us, event | category | flops | bytes accessed | tf_op | source)
XLA Modules:
  0.0 51.7 jit_solution(2297354001538026699)
XLA Ops:
  0.0 50.1 %shard_map.91 = bf16[192,384]{1,0:T(8,128)(2,1)} custom-call(bf16[192,384]{1,0:T(8,128)(2,1)} %frames.1, f32[1536]{0:T(1024)} %attn_gain.1, bf16[3,1536,384]{2,1,0:T(8,128)(2,1)} %qkv.1, bf16[384,1536]{1,0:T(8,128)(2,1)} %out_w.1, f32[1536]{0:T(1024)} %conv_gain.1, bf16[2,1536,384]{2,1,0:T(8,128)(2,1)} %glu_w.1, bf16[31,384]{1,0:T(8,128)(2,1)} %depth_k.1, ...), custom_call_target="tpu_custom_call" | custom-call | tf_op jit(solution)/shard_map/pallas_call | solution.py:696
  50.1 1.6 %copy.11 = bf16[192,384]{1,0:T(8,128)(2,1)} copy(bf16[192,384]{1,0:T(8,128)(2,1)} %shard_map.91) | data formatting | bytes 294912

commit v6 on v5

--- a/solution.py
+++ b/solution.py
@@ -13,6 +13,7 @@
 ROW_CHUNKS = 2
 PARTS = 2
 WINDOW = 256
+SLOT = 128
 MESH = pl.DeviceIdType.MESH
 
 
@@ -155,6 +156,7 @@
     proj_w,
     out,
     w_qkv,
+    w_head,
     w_out,
     w_glu,
     w_proj,
@@ -167,7 +169,9 @@
     normed,
     q_all,
     k_all,
+    k_turned,
     v_all,
+    score_rows,
     context_out,
     context_in,
     part32,
@@ -244,7 +248,15 @@
                 local_sem.at[1 + i],
             )
         )
-    local.append(pltpu.make_async_copy(out_w, w_out, local_sem.at[4]))
+    out_copies = [
+        pltpu.make_async_copy(
+            out_w.at[pl.ds(head * HEAD, HEAD)],
+            w_out.at[pl.ds(head * SLOT, HEAD)],
+            local_sem.at[12 + head],
+        )
+        for head in range(ctx_size)
+    ]
+    local.append(out_copies[0])
     for i in range(2):
         local.append(
             pltpu.make_async_copy(
@@ -256,6 +268,8 @@
     local.append(pltpu.make_async_copy(conv_gain, conv_scale, local_sem.at[9]))
     local.append(pltpu.make_async_copy(depth_b, bias, local_sem.at[10]))
     local.insert(4, pltpu.make_async_copy(attn_gain, attn_scale, local_sem.at[11]))
+
+    local += out_copies[1:]
 
     barrier = pltpu.get_barrier_semaphore()
     for other in (sibling, peer):
@@ -342,11 +356,15 @@
             line += [i for i in (place - hop, place + hop) if 0 <= i < ctx_size]
         order.append(line)
 
-    key_lane = lax.broadcasted_iota(jnp.int32, (rows, WINDOW), 1)
-    in_head = (key_lane >= shift) & (key_lane < shift + HEAD)
-    select_row = lax.broadcasted_iota(jnp.int32, (WINDOW, 128), 0)
-    select_col = lax.broadcasted_iota(jnp.int32, (WINDOW, 128), 1)
+    select_row = lax.broadcasted_iota(jnp.int32, (WINDOW, SLOT), 0)
+    select_col = lax.broadcasted_iota(jnp.int32, (WINDOW, SLOT), 1)
     select = ((select_row == select_col + shift) & (select_col < HEAD)).astype(jnp.bfloat16)
+
+    for i in range(3):
+        local[1 + i].wait()
+        w_head[:, i * SLOT : (i + 1) * SLOT] = jnp.dot(
+            w_qkv[:, i * WINDOW : (i + 1) * WINDOW], select, preferred_element_type=jnp.float32
+        ).astype(jnp.bfloat16)
 
     def project(place):
         index = pick(order, c, place)
@@ -367,14 +385,14 @@
                     store,
                 )
         here = pl.ds(start, rows)
-        projected = jnp.dot(normed[...], w_qkv[...], preferred_element_type=jnp.float32)
-        q_all[here, :] = jnp.where(in_head, projected[:, :WINDOW], 0.0).astype(jnp.bfloat16)
-        k_all[here, :] = projected[:, WINDOW : 2 * WINDOW].astype(jnp.bfloat16)
-        v_all[here, :] = jnp.dot(
-            projected[:, 2 * WINDOW :].astype(jnp.bfloat16),
-            select,
-            preferred_element_type=jnp.float32,
+        projected = jnp.dot(
+            normed[...], w_head[...], preferred_element_type=jnp.float32
         ).astype(jnp.bfloat16)
+        for step in range(ROW_CHUNKS):
+            at = pl.ds(pl.multiple_of(index * step_rows, 16), step_rows)
+            q_all[step, at, :] = projected[step * step_rows : (step + 1) * step_rows, :SLOT]
+        k_all[here, :] = projected[:, SLOT : 2 * SLOT]
+        v_all[here, :] = projected[:, 2 * SLOT :]
 
     def pass_on(hop):
         for part in range(PARTS):
@@ -437,8 +455,8 @@
     pass_on(2)
     pass_side(1)
     from_peer(1)
-    for i in range(5):
-        local[i].wait()
+    local[0].wait()
+    local[4].wait()
     project(0)
     for place in range(2, ctx_size):
         last = place == ctx_size - 1
@@ -457,43 +475,53 @@
     def chunk(step):
         return pl.ds(step * step_rows, step_rows)
 
+    def head_slot(head):
+        return pl.ds(pl.multiple_of(head * SLOT, SLOT), SLOT)
+
     def context_copy(index, step):
         return remote(
             context_out.at[index, chunk(step)],
-            context_in.at[c, chunk(step)],
+            context_in.at[chunk(step), head_slot(c)],
             ctx_send.at[index, step],
             ctx_recv.at[c, step],
             ctx=index,
         )
 
-    def attend(step, place):
-        index = pick(order, c, place)
-        here = pl.ds(pl.multiple_of(index * rows + step * step_rows, 16), step_rows)
-        scores = (
-            lax.dot_general(
-                q_all[here, :],
-                k_all[...],
-                (((1,), (1,)), ((), ())),
-                preferred_element_type=jnp.float32,
-            )
-            * score_scale
-        )
-        weights = jnp.exp(scores - jnp.max(scores, axis=-1, keepdims=True))
-        denominator = jnp.sum(weights, axis=-1, keepdims=True)
+    k_turned[...] = k_all[...].T
+
+    def attend(step, places):
+        indices = [pick(order, c, place) for place in places]
+        rounded, denominators = [], []
+        for index in indices:
+            at = pl.ds(pl.multiple_of(index * step_rows, 16), step_rows)
+            scores = score_rows[at, :] * score_scale
+            weights = jnp.exp(scores - jnp.max(scores, axis=-1, keepdims=True))
+            denominators.append(jnp.sum(weights, axis=-1, keepdims=True))
+            rounded.append(weights.astype(jnp.bfloat16))
         weighted = jnp.dot(
-            weights.astype(jnp.bfloat16), v_all[...], preferred_element_type=jnp.float32
-        )
-        context = (weighted / denominator).astype(jnp.bfloat16)
-        if place:
-            context_out[index, chunk(step), :] = context
-            context_copy(index, step).start()
-        else:
-            context_in[c, chunk(step), :] = context
-
+            jnp.concatenate(rounded, axis=0), v_all[...], preferred_element_type=jnp.float32
+        )
+        for i, (place, index) in enumerate(zip(places, indices)):
+            piece = weighted[i * step_rows : (i + 1) * step_rows] / denominators[i]
+            if place:
+                context_out[index, chunk(step), :] = piece.astype(jnp.bfloat16)
+                context_copy(index, step).start()
+            else:
+                context_in[chunk(step), head_slot(c)] = piece.astype(jnp.bfloat16)
+
+    farthest = list(reversed(range(ctx_size)))
     for step in range(ROW_CHUNKS):
-        for place in reversed(range(ctx_size)):
-            attend(step, place)
-    local[5].wait()
+        score_rows[...] = jnp.dot(
+            q_all[step], k_turned[...], preferred_element_type=jnp.float32
+        )
+        for first in range(0, ctx_size, 2):
+            attend(step, farthest[first : first + 2])
+    for copy in out_copies:
+        copy.wait()
+    for head in range(ctx_size):
+        w_out[head * SLOT + HEAD : (head + 1) * SLOT, :] = jnp.zeros(
+            (SLOT - HEAD, w_out.shape[1]), jnp.bfloat16
+        )
 
     mine = pl.ds(2 * k, 2)
     others = pl.ds(2 * (1 - k), 2)
@@ -516,15 +544,10 @@
     for step in range(ROW_CHUNKS):
         for hop in range(1, ctx_size):
             index = (c + hop) % ctx_size
-            here = context_in.at[index, chunk(step)]
+            here = context_in.at[chunk(step), head_slot(index)]
             remote(here, here, ctx_send.at[index, step], ctx_recv.at[index, step], ctx=index).wait_recv()
-        terms = sum(
-            jnp.dot(
-                context_in[head, chunk(step), :HEAD],
-                w_out[head * HEAD : (head + 1) * HEAD, :],
-                preferred_element_type=jnp.float32,
-            )
-            for head in range(ctx_size)
+        terms = jnp.dot(
+            context_in[chunk(step), :], w_out[...], preferred_element_type=jnp.float32
         )
         for i in range(tp_size):
             piece = terms[:, i * cols : (i + 1) * cols]
@@ -700,7 +723,8 @@
         out_specs=vmem,
         scratch_shapes=[
             pltpu.VMEM((width, 3 * WINDOW), narrow),
-            pltpu.VMEM((cols, width), narrow),
+            pltpu.VMEM((width, 3 * SLOT), narrow),
+            pltpu.VMEM((ctx_size * SLOT, width), narrow),
             pltpu.VMEM((width, 2 * cols), narrow),
             pltpu.VMEM((cols, width), narrow),
             pltpu.VMEM((taps, cols), narrow),
@@ -710,11 +734,13 @@
             pltpu.VMEM((cols,), wide),
             pltpu.VMEM((tp_size, all_rows, cols), narrow),
             pltpu.VMEM((rows, width), narrow),
-            pltpu.VMEM((all_rows, WINDOW), narrow),
-            pltpu.VMEM((all_rows, WINDOW), narrow),
-            pltpu.VMEM((all_rows, 128), narrow),
-            pltpu.VMEM((ctx_size, rows, 128), narrow),
-            pltpu.VMEM((ctx_size, rows, 128), narrow),
+            pltpu.VMEM((ROW_CHUNKS, all_rows // ROW_CHUNKS, SLOT), narrow),
+            pltpu.VMEM((all_rows, SLOT), narrow),
+            pltpu.VMEM((SLOT, all_rows), narrow),
+            pltpu.VMEM((all_rows, SLOT), narrow),
+            pltpu.VMEM((all_rows // ROW_CHUNKS, all_rows), wide),
+            pltpu.VMEM((ctx_size, rows, SLOT), narrow),
+            pltpu.VMEM((rows, ctx_size * SLOT), narrow),
             pltpu.VMEM((tp_size, rows, cols), wide),
             pltpu.VMEM((tp_size, rows, cols), narrow),
             pltpu.VMEM((2, rows, cols), narrow),
@@ -732,7 +758,7 @@
             pltpu.VMEM((rows, cols), wide),
             pltpu.VMEM((rows, cols), narrow),
             pltpu.VMEM((rows, cols), narrow),
-            dma((12,)),
+            dma((12 + ctx_size,)),
             dma((ctx_size, tp_size, PARTS)),
             dma((ctx_size, 2, PARTS)),
             dma((ctx_size, PARTS)),

time: 51.8 us -> 50.9 us (0.983)
  Pallas kernels: 50.1 us -> 49.2 us
    pallas_call x1, Pallas kernels: 50.1 us -> 49.2 us  [fused(): pl.pallas_call(functools.partial(fused_kernel, ctx_size, tp_size), out_sh...]
where the time goes in v6:
time: 50.9 us; the launch traced here: 50.8 us
  Pallas kernels  49.2 us (97%)
  local copies, waits for them, and re-layouts  1.59 us (3%)
    pallas_call x1, Pallas kernels, fused(): pl.pallas_call(functools.partial(fused_kernel, ctx_size, tp_size), out_sh...  49.2 us
    unnamed x1, local copies, waits for them, and re-layouts  1.59 us

profile of v6, /device:TPU:0, one launch (start us, length us, event | category | flops | bytes accessed | tf_op | source)
XLA Modules:
  0.0 50.8 jit_solution(5247175469972113642)
XLA Ops:
  0.0 49.2 %shard_map.91 = bf16[192,384]{1,0:T(8,128)(2,1)} custom-call(bf16[192,384]{1,0:T(8,128)(2,1)} %frames.1, f32[1536]{0:T(1024)} %attn_gain.1, bf16[3,1536,384]{2,1,0:T(8,128)(2,1)} %qkv.1, bf16[384,1536]{1,0:T(8,128)(2,1)} %out_w.1, f32[1536]{0:T(1024)} %conv_gain.1, bf16[2,1536,384]{2,1,0:T(8,128)(2,1)} %glu_w.1, bf16[31,384]{1,0:T(8,128)(2,1)} %depth_k.1, ...), custom_call_target="tpu_custom_call" | custom-call | tf_op jit(solution)/shard_map/pallas_call | solution.py:719
  49.2 1.6 %copy.11 = bf16[192,384]{1,0:T(8,128)(2,1)} copy(bf16[192,384]{1,0:T(8,128)(2,1)} %shard_map.91) | data formatting | bytes 294912

commit v7 on v6

--- a/solution.py
+++ b/solution.py
@@ -195,9 +195,7 @@
     gather_recv,
     sib_send,
     peer_send,
-    up_send,
-    down_send,
-    side_send,
+    along_send,
     ctx_send,
     ctx_recv,
     stage_send,
@@ -304,34 +302,14 @@
             tp=sibling,
         )
 
-    def up(index, part, source):
+    def along(index, part):
         return remote(
-            source,
-            block(index, t, part),
-            up_send.at[index, part],
-            gather_recv.at[index, t, part],
-            ctx=c + 1,
-        )
-
-    def down(index, part, source):
-        return remote(
-            source,
-            block(index, t, part),
-            down_send.at[index, part],
-            gather_recv.at[index, t, part],
-            ctx=c - 1,
-        )
-
-    end = ctx_size - 1
-    late = PARTS - 1
-
-    def side_up():
-        here = block(0, peer, late)
-        return remote(here, here, side_send.at[0], gather_recv.at[0, peer, late], ctx=c + 1)
-
-    def side_down():
-        here = block(end, peer, late)
-        return remote(here, here, side_send.at[1], gather_recv.at[end, peer, late], ctx=c - 1)
+            own_part(part),
+            block(c, t, part),
+            along_send.at[index, part],
+            gather_recv.at[c, t, part],
+            ctx=index,
+        )
 
     def arrived(index, owner, part):
         here = block(index, owner, part)
@@ -343,11 +321,12 @@
     has_down = c > 0
 
     for part in range(PARTS):
-        source = own_part(part)
-        pl.when(has_up)(lambda: up(c, part, source).start())
-        pl.when(has_down)(lambda: down(c, part, source).start())
-        to_peer(c, part, source).start()
-        to_sibling(c, y, part, source).start()
+        to_peer(c, part, own_part(part)).start()
+        to_sibling(c, y, part, own_part(part)).start()
+    for hop in range(1, ctx_size):
+        for part in range(PARTS):
+            pl.when(c >= hop)(lambda: along(c - hop, part).start())
+            pl.when(c + hop < ctx_size)(lambda: along(c + hop, part).start())
 
     order = []
     for place in range(ctx_size):
@@ -394,66 +373,23 @@
         k_all[here, :] = projected[:, SLOT : 2 * SLOT]
         v_all[here, :] = projected[:, 2 * SLOT :]
 
-    def pass_on(hop):
+    def pass_on(place):
+        index = pick(order, c, place)
         for part in range(PARTS):
-
-            @pl.when(c >= hop)
-            def _():
-                index = c - hop
-                arrived(index, t, part)
-                source = block(index, t, part)
-                pl.when(has_up)(lambda: up(index, part, source).start())
-                if part == late:
-                    pl.when(index > 0)(lambda: to_peer(index, part, source).start())
-                else:
-                    to_peer(index, part, source).start()
-                to_sibling(index, y, part, source).start()
-
-            @pl.when(c + hop < ctx_size)
-            def _():
-                index = c + hop
-                arrived(index, t, part)
-                source = block(index, t, part)
-                pl.when(has_down)(lambda: down(index, part, source).start())
-                if part == late:
-                    pl.when(index < end)(lambda: to_peer(index, part, source).start())
-                else:
-                    to_peer(index, part, source).start()
-                to_sibling(index, y, part, source).start()
-
-    def pass_side(hop):
-        @pl.when(c == hop)
-        def _():
-            arrived(0, peer, late)
-            pl.when(has_up)(lambda: side_up().start())
-            to_sibling(0, 1 - y, late, block(0, peer, late)).start()
-
-        @pl.when(c + hop == end)
-        def _():
-            arrived(end, peer, late)
-            pl.when(has_down)(lambda: side_down().start())
-            to_sibling(end, 1 - y, late, block(end, peer, late)).start()
+            arrived(index, t, part)
+            source = block(index, t, part)
+            to_peer(index, part, source).start()
+            to_sibling(index, y, part, source).start()
 
     def from_peer(place):
         index = pick(order, c, place)
-
-        def take(part):
+        for part in range(PARTS):
             arrived(index, peer, part)
             to_sibling(index, 1 - y, part, block(index, peer, part)).start()
 
-        for part in range(PARTS):
-            if part == late and place:
-                pl.when((index > 0) & (index < end))(lambda: take(part))
-            else:
-                take(part)
-        if not place:
-            pl.when(c == 0)(lambda: side_up().start())
-            pl.when(c == end)(lambda: side_down().start())
-
+    from_peer(0)
     pass_on(1)
-    from_peer(0)
     pass_on(2)
-    pass_side(1)
     from_peer(1)
     local[0].wait()
     local[4].wait()
@@ -464,7 +400,6 @@
             pass_on(place + 1)
         else:
             project(place - 1)
-        pass_side(place)
         from_peer(place)
         if not last:
             project(place - 1)
@@ -668,20 +603,13 @@
         ).astype(jnp.bfloat16)
 
     for place in range(ctx_size):
+        index = pick(order, c, place)
         for part in range(PARTS):
-            index = pick(order, c, place)
-            source = block(index, t, part)
-            pl.when(has_up & (index <= c))(lambda: up(index, part, source).wait_send())
-            pl.when(has_down & (index >= c))(lambda: down(index, part, source).wait_send())
-            if part == late:
-                crossed = (index == c) | ((index > 0) & (index < end))
-                pl.when(crossed)(lambda: to_peer(index, part, source).wait_send())
-            else:
-                to_peer(index, part, source).wait_send()
-            to_sibling(index, y, part, source).wait_send()
-            to_sibling(index, 1 - y, part, source).wait_send()
-    pl.when(has_up)(lambda: side_up().wait_send())
-    pl.when(has_down)(lambda: side_down().wait_send())
+            if place:
+                along(index, part).wait_send()
+            to_peer(index, part, block(index, t, part)).wait_send()
+            to_sibling(index, y, part, block(index, t, part)).wait_send()
+            to_sibling(index, 1 - y, part, block(index, t, part)).wait_send()
     for hop in range(1, ctx_size):
         for step in range(ROW_CHUNKS):
             context_copy((c + hop) % ctx_size, step).wait_send()
@@ -763,8 +691,6 @@
             dma((ctx_size, 2, PARTS)),
             dma((ctx_size, PARTS)),
             dma((ctx_size, PARTS)),
-            dma((ctx_size, PARTS)),
-            dma((2,)),
             dma((ctx_size, ROW_CHUNKS)),
             dma((ctx_size, ROW_CHUNKS)),
             dma((5, ROW_CHUNKS)),

time: 50.9 us -> 56 us (1.10)
  Pallas kernels: 49.2 us -> 54.3 us
    pallas_call x1, Pallas kernels: 49.2 us -> 54.3 us  [fused(): pl.pallas_call(functools.partial(fused_kernel, ctx_size, tp_size), out_sh...]
where the time goes in v7:
time: 56 us; the launch traced here: 55.9 us
  Pallas kernels  54.3 us (97%)
  local copies, waits for them, and re-layouts  1.59 us (3%)
    pallas_call x1, Pallas kernels, fused(): pl.pallas_call(functools.partial(fused_kernel, ctx_size, tp_size), out_sh...  54.3 us
    unnamed x1, local copies, waits for them, and re-layouts  1.59 us

profile of v7, /device:TPU:0, one launch (start us, length us, event | category | flops | bytes accessed | tf_op | source)
XLA Modules:
  0.0 55.9 jit_solution(13124576493865528559)
XLA Ops:
  0.0 54.3 %shard_map.91 = bf16[192,384]{1,0:T(8,128)(2,1)} custom-call(bf16[192,384]{1,0:T(8,128)(2,1)} %frames.1, f32[1536]{0:T(1024)} %attn_gain.1, bf16[3,1536,384]{2,1,0:T(8,128)(2,1)} %qkv.1, bf16[384,1536]{1,0:T(8,128)(2,1)} %out_w.1, f32[1536]{0:T(1024)} %conv_gain.1, bf16[2,1536,384]{2,1,0:T(8,128)(2,1)} %glu_w.1, bf16[31,384]{1,0:T(8,128)(2,1)} %depth_k.1, ...), custom_call_target="tpu_custom_call" | custom-call | tf_op jit(solution)/shard_map/pallas_call | solution.py:647
  54.3 1.6 %copy.11 = bf16[192,384]{1,0:T(8,128)(2,1)} copy(bf16[192,384]{1,0:T(8,128)(2,1)} %shard_map.91) | data formatting | bytes 294912
